TPU v7x, 512 devices: a whole 4x8x8 slice. The times are simulated.
512 devices in a mesh: blk: 16 (over y, x_lo), rep: 32 (over z, x_hi, core).
Axes of the slice: x: 4 (x_hi: 2, x_lo: 2; x = x_hi * 2 + x_lo), y: 8, z: 8, core: 2. Of those that a mesh axis runs over, the one named last changes fastest.
Arguments:
- hamiltonian: float32 [3072, 64, 768], P(('blk', 'rep')), as said below
- pattern: int32 [3072, 12], P(('blk', 'rep')), may hold values from 0 to 1, as said below
Outputs:
- sign_matrix: float32 [3072, 64, 768], P(('blk', 'rep'))
Inputs may be any that keep to these rules, and one draw needn't show every extreme that they name: pattern is symmetric: pattern[i, 6 + w] equals pattern[i + w, 6 - w] (block indices modulo 3072); the diagonal position 6 is always 1 and position 0 always 0. hamiltonian is symmetric in the sense of its meaning, and block position 0 is zero.
All inputs are finite; a program needn't handle non-finite values.
Results may differ from a plain program's by a relative error of at most 0.0001.
Values sent between devices are 32-bit elements; how exact they have to be, the bound alone decides.
No kernel may reach another device: no remote copies, remote signals or barrier semaphores. Data moves between devices by JAX's collectives and lax.ppermute only.
A program may use at most 128 MiB of HBM per device.

v0:
```python
import math

import jax
import jax.numpy as jnp
from jax import lax
from jax.sharding import PartitionSpec as P

BS = 64
HALF = 6
ITERS = 2


def from_behind(block, axis, distance):
    devices = range(lax.axis_size(axis))
    route = [((i - distance) % len(devices), i) for i in devices]
    return lax.ppermute(block, axis, route)


def extend(right_band):
    local_rows = right_band.shape[0]
    from_below = from_behind(right_band, ("blk", "rep"), 1)
    from_above = from_behind(right_band[: HALF - 1], ("blk", "rep"), -1)
    return jnp.concatenate([from_below, right_band, from_above], axis=0)


def band_product(left_band, extended, pattern_cols):
    local_rows = left_band.shape[0]
    outputs = []
    for position in range(2 * HALF):
        out_offset = position - HALF
        first_u = max(-HALF, out_offset - HALF + 1)
        last_u = min(HALF - 1, out_offset + HALF)
        factor = left_band[:, :, (first_u + HALF) * BS : (last_u + HALF + 1) * BS]
        pieces = []
        for inner in range(first_u, last_u + 1):
            column = (out_offset - inner + HALF) * BS
            pieces.append(
                extended[HALF + inner : HALF + inner + local_rows, :, column : column + BS]
            )
        stacked = jnp.concatenate(pieces, axis=1)
        block_out = jnp.einsum("rak,rkc->rac", factor, stacked, precision=lax.Precision.HIGHEST)
        outputs.append(block_out * pattern_cols[:, position][:, None, None])
    return jnp.concatenate(outputs, axis=2)


def local(hamiltonian, pattern):
    pattern_cols = pattern.astype(jnp.float32)
    mask_cols = jnp.repeat(pattern_cols, BS, axis=1)[:, None, :]
    masked = hamiltonian * mask_cols
    total_rows = lax.axis_size(("blk", "rep")) * masked.shape[0]
    frob_norm = jnp.sqrt(lax.psum(jnp.sum(masked * masked), ("blk", "rep")))
    scaling = math.sqrt(total_rows * BS) / (3.0 * frob_norm)
    current = scaling * masked
    square = band_product(current, extend(current), pattern_cols)
    for iteration in range(ITERS):
        if iteration > 0:
            square = band_product(current, extend(current), pattern_cols)
        cubic = band_product(current, extend(square), pattern_cols)
        current = 0.5 * (3.0 * current - cubic)
    return current / scaling


def solution(mesh):
    placed = (P(("blk", "rep"), None, None), P(("blk", "rep"), None))
    return jax.shard_map(
        local, mesh=mesh, in_specs=placed, out_specs=P(("blk", "rep"), None, None), check_vma=False
    )
```

profile of v0, /device:TPU:195, one launch (start us, length us, event | category | flops | bytes accessed | tf_op | source)
XLA Modules:
  0.0 552.9 jit_solution(3415120405039094413)
XLA Ops:
  4.1 99.2 %psum.7 = f32[]{:T(128)} all-reduce(f32[]{:T(128)} %multiply_reduce_fusion), channel_id=1, replica_groups=mesh['blk'=16,'rep'=32] {'blk','rep'}, use_global_device_ids=true, to_apply=%region_1.0 | all-reduce | flops 1 | bytes 8 | tf_op jit(solution)/shard_map/psum | solution.py:51
  107.5 3.1 copy.108
  114.8 4.5 collective-permute-start
  121.1 19.3 %collective-permute-done.1 = f32[5,64,768]{2,1,0:T(8,128)} collective-permute-done((f32[5,64,768]{2,1,0:T(8,128)}, f32[5,64,768]{2,1,0:T(8,128)}, u32[]{:S(2)}, u32[]{:S(2)}) %collective-permute-start.1) | collective-permute-done | bytes 983072 | tf_op jit(solution)/shard_map/ppermute | solution.py:16
  140.4 3.1 copy.109
  216.3 3.1 copy.142
  224.1 5.1 collective-permute-start.2
  229.3 20.0 %collective-permute-done.3 = f32[5,64,768]{2,1,0:T(8,128)} collective-permute-done((f32[5,64,768]{2,1,0:T(8,128)}, f32[5,64,768]{2,1,0:T(8,128)}, u32[]{:S(2)}, u32[]{:S(2)}) %collective-permute-start.3) | collective-permute-done | bytes 983072 | tf_op jit(solution)/shard_map/ppermute | solution.py:16
  249.2 3.1 copy.143
  265.3 3.0 pad_maximum_fusion.5
  298.1 3.0 fusion.155
  328.1 3.1 copy.176
  334.8 5.1 collective-permute-start.4
  340.8 20.3 %collective-permute-done.5 = f32[5,64,768]{2,1,0:T(8,128)} collective-permute-done((f32[5,64,768]{2,1,0:T(8,128)}, f32[5,64,768]{2,1,0:T(8,128)}, u32[]{:S(2)}, u32[]{:S(2)}) %collective-permute-start.5) | collective-permute-done | bytes 983072 | tf_op jit(solution)/shard_map/ppermute | solution.py:16
  361.0 3.1 copy.177
  406.4 3.0 constant_dynamic-update-slice_fusion.19
  411.4 3.1 constant_dynamic-update-slice_fusion.18
  416.7 3.1 constant_dynamic-update-slice_fusion.17
  440.3 3.1 copy.210
  448.0 5.1 collective-permute-start.6
  453.2 19.7 %collective-permute-done.7 = f32[5,64,768]{2,1,0:T(8,128)} collective-permute-done((f32[5,64,768]{2,1,0:T(8,128)}, f32[5,64,768]{2,1,0:T(8,128)}, u32[]{:S(2)}, u32[]{:S(2)}) %collective-permute-start.7) | collective-permute-done | bytes 983072 | tf_op jit(solution)/shard_map/ppermute | solution.py:16
  472.9 3.1 copy.211
  521.6 3.0 fusion.153
  526.8 3.0 fusion.261
  (269 shorter events, 306.6 us)
Async XLA Ops:
  2.5 101.4 %copy-start.12 = (f32[6,64,768]{1,2,0:T(8,128)}, f32[6,64,768]{1,2,0:T(8,128)S(1)}, u32[]{:S(2)}) copy-start(f32[6,64,768]{1,2,0:T(8,128)S(1)} %copy.101) | copy-start | bytes 3538948
  2.7 103.4 %copy-start.39 = (f32[6,768]{1,0:T(8,128)}, f32[6,768]{1,0:T(8,128)S(1)}, u32[]{:S(2)}) copy-start(f32[6,768]{1,0:T(8,128)S(1)} %mul.168) | copy-start | bytes 55300
  110.6 29.9 %collective-permute-start.1 = (f32[5,64,768]{2,1,0:T(8,128)}, f32[5,64,768]{2,1,0:T(8,128)}, u32[]{:S(2)}, u32[]{:S(2)}) collective-permute-start(f32[5,64,768]{2,1,0:T(8,128)} %copy.108), channel_id=1, source_target_pairs={{1,0},{2,1},{3,2},{4,3},{5,4},{6,5},{7,6},{8,7},{9,8},{10,9},{11,1... | collective-permute-start | bytes 2949128 | tf_op jit(solution)/shard_map/ppermute | solution.py:16
  114.8 39.0 %collective-permute-start = (f32[6,64,768]{2,1,0:T(8,128)}, f32[6,64,768]{2,1,0:T(8,128)S(1)}, u32[]{:S(2)}, u32[]{:S(2)}) collective-permute-start(f32[6,64,768]{2,1,0:T(8,128)} %copy.102), channel_id=1, source_target_pairs={{511,0},{0,1},{1,2},{2,3},{3,4},{4,5},{5,6},{6,7},{7,8},{8,9},{9,1... | collective-permute-start | bytes 3538952 | tf_op jit(solution)/shard_map/ppermute | solution.py:16
  171.5 4.3 copy-start.43
  197.6 4.7 copy-start.42
  219.4 29.9 %collective-permute-start.3 = (f32[5,64,768]{2,1,0:T(8,128)}, f32[5,64,768]{2,1,0:T(8,128)}, u32[]{:S(2)}, u32[]{:S(2)}) collective-permute-start(f32[5,64,768]{2,1,0:T(8,128)} %copy.142), channel_id=1, source_target_pairs={{1,0},{2,1},{3,2},{4,3},{5,4},{6,5},{7,6},{8,7},{9,8},{10,9},{11,1... | collective-permute-start | bytes 2949128 | tf_op jit(solution)/shard_map/ppermute | solution.py:16
  224.1 39.2 %collective-permute-start.2 = (f32[6,64,768]{2,1,0:T(8,128)}, f32[6,64,768]{2,1,0:T(8,128)S(1)}, u32[]{:S(2)}, u32[]{:S(2)}) collective-permute-start(f32[6,64,768]{2,1,0:T(8,128)} %copy.136), channel_id=1, source_target_pairs={{511,0},{0,1},{1,2},{2,3},{3,4},{4,5},{5,6},{6,7},{7,8},{8,9},{9,1... | collective-permute-start | bytes 3538952 | tf_op jit(solution)/shard_map/ppermute | solution.py:16
  274.5 4.0 copy-start.32
  282.1 4.6 copy-start.28
  306.3 4.7 copy-start.35
  319.9 4.6 copy-start.13
  319.9 4.5 copy-start.40
  331.1 29.9 %collective-permute-start.5 = (f32[5,64,768]{2,1,0:T(8,128)}, f32[5,64,768]{2,1,0:T(8,128)}, u32[]{:S(2)}, u32[]{:S(2)}) collective-permute-start(f32[5,64,768]{2,1,0:T(8,128)} %copy.176), channel_id=1, source_target_pairs={{1,0},{2,1},{3,2},{4,3},{5,4},{6,5},{7,6},{8,7},{9,8},{10,9},{11,1... | collective-permute-start | bytes 2949128 | tf_op jit(solution)/shard_map/ppermute | solution.py:16
  334.8 39.5 %collective-permute-start.4 = (f32[6,64,768]{2,1,0:T(8,128)}, f32[6,64,768]{2,1,0:T(8,128)S(1)}, u32[]{:S(2)}, u32[]{:S(2)}) collective-permute-start(f32[6,64,768]{2,1,0:T(8,128)} %copy.170), channel_id=1, source_target_pairs={{511,0},{0,1},{1,2},{2,3},{3,4},{4,5},{5,6},{6,7},{7,8},{8,9},{9,1... | collective-permute-start | bytes 3538952 | tf_op jit(solution)/shard_map/ppermute | solution.py:16
  386.8 4.2 copy-start.30
  386.8 4.2 copy-start.38
  395.2 4.6 copy-start.26
  443.3 29.6 %collective-permute-start.7 = (f32[5,64,768]{2,1,0:T(8,128)}, f32[5,64,768]{2,1,0:T(8,128)}, u32[]{:S(2)}, u32[]{:S(2)}) collective-permute-start(f32[5,64,768]{2,1,0:T(8,128)} %copy.210), channel_id=1, source_target_pairs={{1,0},{2,1},{3,2},{4,3},{5,4},{6,5},{7,6},{8,7},{9,8},{10,9},{11,1... | collective-permute-start | bytes 2949128 | tf_op jit(solution)/shard_map/ppermute | solution.py:16
  448.0 38.8 %collective-permute-start.6 = (f32[6,64,768]{2,1,0:T(8,128)}, f32[6,64,768]{2,1,0:T(8,128)S(1)}, u32[]{:S(2)}, u32[]{:S(2)}) collective-permute-start(f32[6,64,768]{2,1,0:T(8,128)} %copy.204), channel_id=1, source_target_pairs={{511,0},{0,1},{1,2},{2,3},{3,4},{4,5},{5,6},{6,7},{7,8},{8,9},{9,1... | collective-permute-start | bytes 3538952 | tf_op jit(solution)/shard_map/ppermute | solution.py:16
  505.5 4.6 copy-start.27
  529.8 4.7 copy-start.33
  543.4 4.6 copy-start.14
  543.4 4.6 copy-start.41
  (37 other events, 108.3 us)
where the time goes:
time: 560 us; the launch traced here: 553 us
  local copies, waits for them, and re-layouts  153 us (27%)
  matrix products  118 us (21%)
  blocking collectives  99.2 us (18%)
  waiting for transfers between devices  79.3 us (14%)
  other arithmetic  73.3 us (13%)
  starting transfers between devices  28.2 us (5%)
    dot_general x48, matrix products, band_product(): jnp.einsum('rak,rkc->rac', factor, stacked, precision=lax.Precision.HIGHEST)  118 us
    psum x1, blocking collectives, local(): frob_norm = jnp.sqrt(lax.psum(jnp.sum(masked * masked), ('blk', 'rep')))  99.2 us
    concatenate x48, local copies, waits for them, and re-layouts, band_product(): stacked = jnp.concatenate(pieces, axis=1)  88.7 us
    ppermute x8, waiting for transfers between devices, from_behind(): return lax.ppermute(block, axis, route)  79.3 us
    concatenate x40, other arithmetic, extend(): return jnp.concatenate([from_below, right_band, from_above], axis=0)  64.3 us
    ppermute x8, starting transfers between devices, from_behind(): return lax.ppermute(block, axis, route)  28.2 us
    slice x8, local copies, waits for them, and re-layouts, extend(): from_above = from_behind(right_band[:HALF - 1], ('blk', 'rep'), -1)  21.2 us
    ppermute x8, local copies, waits for them, and re-layouts, from_behind(): return lax.ppermute(block, axis, route)  20.9 us
  transfers between devices with their start and end apart: 8, of which 4 were waited for; matrix products, arithmetic and copies ran while one was open for 12% of the time, Pallas kernels for 0%

commit v1 on v0

v1 whole, which is shorter than its diff:
```python
import math

import jax
import jax.numpy as jnp
from jax import lax
from jax.experimental import pallas as pl
from jax.experimental.pallas import tpu as pltpu
from jax.sharding import PartitionSpec as P

BS = 64
AXES = ("blk", "rep")
F32 = jnp.float32
BF16 = jnp.bfloat16
VMEM = pl.BlockSpec(memory_space=pltpu.VMEM)
HBM = pl.BlockSpec(memory_space=pltpu.HBM)


def shift(block, distance):
    n = lax.axis_size(AXES)
    return lax.ppermute(block, AXES, [(i, (i + distance) % n) for i in range(n)])


def zeros(rows, blocks):
    return jnp.zeros((rows, blocks * BS), F32)


def lanes(*parts):
    return jnp.concatenate([p for p in parts if p.shape[1]], axis=1)


def split(x):
    high = x.astype(BF16)
    return high, (x - high.astype(F32)).astype(BF16)


def dot(a, b):
    return lax.dot_general(a, b, (((1,), (0,)), ((), ())), preferred_element_type=F32)


def dot3(a_high, a_low, b_high, b_low):
    return dot(a_high, b_high) + (dot(a_high, b_low) + dot(a_low, b_high))


def put(ref_high, ref_low, start, value):
    high, low = split(value)
    ref_high[start : start + value.shape[0], :] = high
    ref_low[start : start + value.shape[0], :] = low


def masked_rows(x, mask):
    pieces = [
        x[BS * i : BS * (i + 1)] * mask[i : i + 1] for i in range(x.shape[0] // BS)
    ]
    return jnp.concatenate(pieces, axis=0)


def prepare_kernel(h_ref, pat_ref, m_ref, mask_ref, right_ref, left_ref, right2_ref, left2_ref, ssq_ref):
    pat = pat_ref[...].astype(F32)
    owner = lax.broadcasted_iota(jnp.int32, (12, 12 * BS), 1) // BS
    spread = (owner == lax.broadcasted_iota(jnp.int32, (12, 12 * BS), 0)).astype(F32)
    mask = dot(pat, spread)
    mask = jnp.concatenate([mask, jnp.zeros((2, 12 * BS), F32)], axis=0)
    mask_ref[...] = mask
    total = jnp.zeros((8, 128), F32)
    rows = []
    for i in range(6):
        at = slice(BS * i, BS * (i + 1))
        row = h_ref[at, :] * mask[i : i + 1, :]
        m_ref[at, :] = row
        right_ref[at, :] = row[:, 64:448]
        left_ref[at, :] = row[:, 384:768]
        square = row * row
        for a in range(8):
            for b in range(6):
                total = total + square[8 * a : 8 * a + 8, 128 * b : 128 * b + 128]
        rows.append(row)
    upper = lanes(mask[:, 448:768], zeros(8, 1))
    for ref in (right_ref, left_ref):
        ref[384:392, :] = mask[:, 64:448]
        ref[392:400, :] = upper
    right2_ref[...] = lanes(rows[5][:, 192:448], rows[4][:, 256:448], rows[2][:, 384:448], rows[3][:, 320:448])
    left2_ref[...] = lanes(rows[0][:, 384:640], rows[1][:, 384:576], rows[3][:, 384:448], rows[2][:, 384:512])
    ssq_ref[...] = jnp.zeros(ssq_ref.shape, F32) + jnp.sum(total)


def spread_sum_kernel(in_ref, out_ref):
    out_ref[...] = jnp.zeros(out_ref.shape, F32) + jnp.sum(in_ref[...]) / 128.0


def own_window(x):
    n = x.shape[0] // 6 if x.shape[0] > 8 else 1
    out = []
    for i in range(6):
        row = x[n * i : n * (i + 1)]
        if i == 0:
            out.append(lanes(row[:, BS:], zeros(n, 5)))
        else:
            out.append(lanes(zeros(n, i - 1), row, zeros(n, 5 - i)))
    return jnp.concatenate(out, axis=0)


def mirror(a, lower):
    br = lax.broadcasted_iota(jnp.int32, a.shape, 0) // BS
    bc = lax.broadcasted_iota(jnp.int32, a.shape, 1) // BS
    keep = br >= bc if lower else br <= bc
    return jnp.where(keep, a, a.T)


def first_kernel(
    m_ref, mask_ref, fl_ref, fr_ref, fl2_ref, fr2_ref,
    mo_ref, ml_ref, mr_ref, to_ref, tl_ref, tr_ref, ko_ref, kl_ref, kr_ref, g_ref,
    lh, ll, oh, ol, rh, rl,
):
    top = jnp.maximum(jnp.max(jnp.abs(m_ref[...])), jnp.max(jnp.abs(fl_ref[0:384, :])))
    top = jnp.maximum(top, jnp.max(jnp.abs(fr_ref[0:384, :])))
    top = jnp.maximum(top, jnp.max(jnp.abs(fl2_ref[...])))
    top = jnp.maximum(top, jnp.max(jnp.abs(fr2_ref[...])))
    top = jnp.maximum(top, 1e-30)
    g = 1.0 / top
    g_ref[...] = jnp.zeros(g_ref.shape, F32) + top

    fl = fl_ref[0:384, :] * g
    fr = fr_ref[0:384, :] * g
    fl2 = fl2_ref[...] * g
    fr2 = fr2_ref[...] * g
    a = [
        lanes(fl2[:, 448:512], zeros(BS, 9)),
        lanes(fl2[:, 512:640], zeros(BS, 8)),
        lanes(fl2[:, 256:448], zeros(BS, 7)),
        lanes(fl2[:, 0:256], zeros(BS, 6)),
        lanes(fl[0:64, 64:384], zeros(BS, 5)),
    ]
    for i in range(1, 6):
        a.append(lanes(zeros(BS, i - 1), fl[64 * i : 64 * i + 64], zeros(BS, 5 - i)))
    full_l = mirror(jnp.concatenate(a, axis=0), True)
    a = []
    for i in range(5):
        a.append(lanes(zeros(BS, i), fr[64 * i : 64 * i + 64], zeros(BS, 4 - i)))
    a.append(lanes(zeros(BS, 5), fr[320:384, 0:320]))
    a.append(lanes(zeros(BS, 6), fr2[:, 0:256]))
    a.append(lanes(zeros(BS, 7), fr2[:, 256:448]))
    a.append(lanes(zeros(BS, 8), fr2[:, 512:640]))
    a.append(lanes(zeros(BS, 9), fr2[:, 448:512]))
    full_r = mirror(jnp.concatenate(a, axis=0), False)
    own = own_window(m_ref[...] * g)
    cross_l = own[:, 0:384].T[0:320]
    cross_r = own[:, 640:1024].T[64:384]
    halo_l = lanes(zeros(320, 1), full_l[320:640], cross_l[:, 0:320])
    halo_r = lanes(cross_r[:, 64:384], full_r[0:320], zeros(320, 1))
    halo_lo = lanes(full_l[320:640, 320:640], cross_l, zeros(320, 5))
    halo_ro = lanes(zeros(320, 5), cross_r, full_r[0:320, 0:320])
    mo_ref[...] = own
    ml_ref[...] = halo_lo[:, 0:640]
    mr_ref[...] = halo_ro[:, 384:1024]

    put(lh, ll, 0, zeros(64, 16))
    put(lh, ll, 64, lanes(zeros(320, 1), full_l[0:320], zeros(320, 5)))
    put(lh, ll, 384, halo_l)
    put(lh, ll, 704, lanes(zeros(320, 6), own[0:320, 0:640]))
    put(oh, ol, 0, halo_lo)
    put(oh, ol, 320, own)
    put(oh, ol, 704, halo_ro)
    put(rh, rl, 0, lanes(own[64:384, 384:1024], zeros(320, 6)))
    put(rh, rl, 320, halo_r)
    put(rh, rl, 640, lanes(zeros(320, 5), full_r[320:640], zeros(320, 1)))
    put(rh, rl, 960, zeros(64, 16))

    mask_o = own_window(mask_ref[...])
    ko_ref[...] = jnp.concatenate([mask_o, jnp.zeros((2, 1024), F32)], axis=0)
    mask_l, mask_r = [], []
    for i in range(5):
        band = lanes(fl_ref[385 + i : 386 + i, :], fl_ref[393 + i : 394 + i, 0:320])
        mask_l.append(lanes(zeros(1, 1 + i), band, zeros(1, 4 - i)))
        band = lanes(fr_ref[384 + i : 385 + i, :], fr_ref[392 + i : 393 + i, 0:320])
        mask_r.append(lanes(zeros(1, i), band, zeros(1, 5 - i)))
    mask_l = jnp.concatenate(mask_l, axis=0)
    mask_r = jnp.concatenate(mask_r, axis=0)
    pad = jnp.zeros((3, 640), F32)
    kl_ref[...] = jnp.concatenate([mask_l[:, 384:1024], pad], axis=0)
    kr_ref[...] = jnp.concatenate([mask_r[:, 0:640], pad], axis=0)

    s_l = masked_rows(dot3(lh[384:704, :], ll[384:704, :], lh[...], ll[...]), mask_l)
    s_o = masked_rows(dot3(oh[320:704, :], ol[320:704, :], oh[...], ol[...]), mask_o)
    s_r = masked_rows(dot3(rh[320:640, :], rl[320:640, :], rh[...], rl[...]), mask_r)

    ah, al = lh[384:704, :], ll[384:704, :]
    s_left = jnp.concatenate(
        [zeros(64, 10), lanes(s_l[:, 0:384].T[64:384], zeros(320, 5)), s_l[:, 384:1024], s_o[0:320, 0:640]], axis=0
    )
    tl_ref[...] = masked_rows(dot3(ah, al, *split(s_left)), mask_l[:, 384:1024])
    ah, al = rh[320:640, :], rl[320:640, :]
    s_right = jnp.concatenate(
        [s_o[64:384, 384:1024], s_r[:, 0:640], lanes(zeros(320, 5), s_r[:, 640:1024].T[0:320]), zeros(64, 10)], axis=0
    )
    tr_ref[...] = masked_rows(dot3(ah, al, *split(s_right)), mask_r[:, 0:640])
    ah, al = oh[320:704, :], ol[320:704, :]
    s_mid = jnp.concatenate(
        [lanes(s_l[:, 384:1024], zeros(320, 6)), s_o, lanes(zeros(320, 6), s_r[:, 0:640])], axis=0
    )
    to_ref[...] = masked_rows(dot3(ah, al, *split(s_mid)), mask_o)


def second_kernel(
    norms_ref, g_ref, mo_ref, ml_ref, mr_ref, to_ref, tl_ref, tr_ref, ko_ref,
    x_ref, xh, xl, s2_ref, right_ref, left_ref, inv_ref, *, size
):
    frob = jnp.sqrt(jnp.sum(norms_ref[...], keepdims=True)[0] / 128.0)
    inverse = 3.0 * frob / size
    inv_ref[...] = jnp.zeros(inv_ref.shape, F32) + inverse
    r = g_ref[0:1, 0:1] / inverse
    c1 = 1.5 * r
    c3 = 0.5 * r * r * r
    x_o = c1 * mo_ref[...] - c3 * to_ref[...]
    x_ref[...] = x_o
    put(xh, xl, 0, lanes(c1 * ml_ref[...] - c3 * tl_ref[...], zeros(320, 6)))
    put(xh, xl, 320, x_o)
    put(xh, xl, 704, lanes(zeros(320, 6), c1 * mr_ref[...] - c3 * tr_ref[...]))
    s2 = dot3(xh[320:704, :], xl[320:704, :], xh[:, 256:768], xl[:, 256:768])
    s2 = masked_rows(s2, ko_ref[0:6, 256:768])
    s2_ref[...] = s2
    for ref, block in ((right_ref, s2[64:384, 128:448]), (left_ref, s2[0:320, 64:384])):
        ref[0:320, :] = block[:, 0:128]
        ref[320:640, :] = block[:, 128:256]
        ref[640:800, :] = lanes(block[0:160, 256:320], block[160:320, 256:320])


def third_kernel(xh, xl, s2_ref, ko_ref, kl_ref, kr_ref, out_ref):
    ah, al = xh[320:704, :], xl[320:704, :]
    s2_a = masked_rows(dot3(ah, al, xh[:, 0:256], xl[:, 0:256]), ko_ref[0:6, 0:256])
    s2_b = masked_rows(dot3(ah, al, xh[:, 768:1024], xl[:, 768:1024]), ko_ref[0:6, 768:1024])
    s2_l = dot3(xh[0:320, 0:640], xl[0:320, 0:640], xh[0:640, 256:640], xl[0:640, 256:640])
    s2_l = masked_rows(s2_l, kl_ref[0:5, 256:640])[:, 64:384]
    s2_r = dot3(xh[704:1024, 384:1024], xl[704:1024, 384:1024], xh[384:1024, 384:768], xl[384:1024, 384:768])
    s2_r = masked_rows(s2_r, kr_ref[0:5, 0:384])[:, 0:320]
    s2 = jnp.concatenate(
        [
            lanes(zeros(320, 5), s2_l, zeros(320, 6)),
            lanes(s2_a, s2_ref[...], s2_b),
            lanes(zeros(320, 6), s2_r, zeros(320, 5)),
        ],
        axis=0,
    )
    out_ref[...] = dot3(ah, al, *split(s2))


def unpack(ref):
    tail = ref[640:800, :]
    return lanes(ref[0:320, :], ref[320:640, :], jnp.concatenate([tail[:, 0:64], tail[:, 64:128]], axis=0))


def last_kernel(part_ref, x_ref, xh, xl, ko_ref, inv_ref, fl_ref, fr_ref, out_ref):
    corner_l = jnp.concatenate([lanes(unpack(fl_ref), zeros(320, 1)), zeros(64, 6)], axis=0)
    corner_r = jnp.concatenate([zeros(64, 6), lanes(zeros(320, 1), unpack(fr_ref))], axis=0)
    add_l = dot3(xh[320:704, 0:384], xl[320:704, 0:384], *split(corner_l))
    add_r = dot3(xh[320:704, 640:1024], xl[320:704, 640:1024], *split(corner_r))
    cubic = lanes(part_ref[:, 0:384] + add_l, part_ref[:, 384:640], part_ref[:, 640:1024] + add_r)
    inverse = inv_ref[0:1, 0:1]
    for i in range(6):
        at = slice(BS * i, BS * (i + 1))
        row = (1.5 * x_ref[at, :] - 0.5 * (cubic[at] * ko_ref[i : i + 1, :])) * inverse
        if i == 0:
            out_ref[at, :] = lanes(zeros(BS, 1), row[:, 0:704])
        else:
            out_ref[at, :] = row[:, 64 * (i - 1) : 64 * (i - 1) + 768]


def call(kernel, outs, args, flops, name, scratch=(), spaces=None):
    return pl.pallas_call(
        kernel,
        out_shape=[jax.ShapeDtypeStruct(s, t) for s, t in outs],
        in_specs=[VMEM] * len(args),
        out_specs=spaces or [VMEM] * len(outs),
        scratch_shapes=list(scratch),
        compiler_params=pltpu.CompilerParams(vmem_limit_bytes=48 << 20),
        cost_estimate=pl.CostEstimate(flops=flops, bytes_accessed=1 << 20, transcendentals=0),
        name=name,
    )(*args)


def local(hamiltonian, pattern):
    n_blk, n_rep = lax.axis_size("blk"), lax.axis_size("rep")
    size = math.sqrt(n_blk * n_rep * 6 * BS)
    band = hamiltonian.reshape(6 * BS, 12 * BS)
    m, mask, to_right, to_left, to_right2, to_left2, ssq = call(
        prepare_kernel,
        [((384, 768), F32), ((8, 768), F32), ((400, 384), F32), ((400, 384), F32),
         ((64, 640), F32), ((64, 640), F32), ((n_rep, 1, 128), F32)],
        (band, pattern), 10**7, "prepare",
    )
    from_left = shift(to_right, 1)
    from_right = shift(to_left, -1)
    from_left2 = shift(to_right2, 2)
    from_right2 = shift(to_left2, -2)
    ssq = lax.all_to_all(ssq, "rep", 0, 0)
    (ssq,) = call(spread_sum_kernel, [((n_blk, 1, 128), F32)], (ssq,), 10**5, "row_sum")
    ssq = lax.all_to_all(ssq, "blk", 0, 0)
    wide = pltpu.VMEM((1024, 1024), BF16)
    big, halo = ((384, 1024), F32), ((320, 640), F32)
    mo, ml, mr, to, tl, tr, ko, kl, kr, g = call(
        first_kernel,
        [big, halo, halo, big, halo, halo, ((8, 1024), F32), ((8, 640), F32), ((8, 640), F32), ((8, 128), F32)],
        (m, mask, from_left, from_right, from_left2, from_right2), 10**10, "first_iteration",
        scratch=[wide] * 6,
    )
    x, xh, xl, s2, to_right, to_left, inverse = call(
        lambda *refs: second_kernel(*refs, size=size),
        [big, ((1024, 1024), BF16), ((1024, 1024), BF16), ((384, 512), F32),
         ((800, 128), F32), ((800, 128), F32), ((8, 128), F32)],
        (ssq, g, mo, ml, mr, to, tl, tr, ko), 10**9, "second_square",
    )
    from_left = shift(to_right, 1)
    from_right = shift(to_left, -1)
    (part,) = call(third_kernel, [big], (xh, xl, s2, ko, kl, kr), 10**10, "second_cubic")
    (out,) = call(
        last_kernel, [((384, 768), F32)], (part, x, xh, xl, ko, inverse, from_left, from_right), 10**9, "result"
    )
    return out.reshape(6, BS, 12 * BS)


def solution(mesh):
    placed = (P(AXES, None, None), P(AXES, None))
    return jax.shard_map(
        local, mesh=mesh, in_specs=placed, out_specs=P(AXES, None, None), check_vma=False
    )
```

time: 560 us -> 104 us (0.19)
  the two profiles are of different devices: /device:TPU:195 before, /device:TPU:1 now
where the time goes in v1:
time: 104 us; the launch traced here: 103 us
  starting transfers between devices  33.9 us (33%)
  Pallas kernels  33.7 us (32%)
  blocking collectives  19.3 us (19%)
  local copies, waits for them, and re-layouts  11.2 us (11%)
  waiting for transfers between devices  4.65 us (4%)
    pallas_call x6, Pallas kernels, call(): pl.pallas_call(kernel, out_shape=[jax.ShapeDtypeStruct(s, t) for s, t in...  33.7 us
    ppermute x6, starting transfers between devices, shift(): lax.ppermute(block, AXES, [(i, (i + distance) % n) for i in range(n)])  28.6 us
    all_to_all x1, blocking collectives, local(): ssq = lax.all_to_all(ssq, 'rep', 0, 0)  19.3 us
    unnamed x26, local copies, waits for them, and re-layouts  11.2 us
    all_to_all x1, starting transfers between devices, local(): ssq = lax.all_to_all(ssq, 'blk', 0, 0)  5.29 us
    ppermute x6, waiting for transfers between devices, shift(): lax.ppermute(block, AXES, [(i, (i + distance) % n) for i in range(n)])  4.65 us
  transfers between devices with their start and end apart: 7, of which 1 were waited for; matrix products, arithmetic and copies ran while one was open for 0% of the time, Pallas kernels for 22%

profile of v1, /device:TPU:1, one launch (start us, length us, event | category | flops | bytes accessed | tf_op | source)
XLA Modules:
  0.0 102.9 jit_solution(6420162098347173023)
XLA Ops:
  0.0 1.3 %copy-done.3 = f32[6,64,768]{2,1,0:T(8,128)S(1)} copy-done((f32[6,64,768]{2,1,0:T(8,128)S(1)}, f32[6,64,768]{2,1,0:T(8,128)}, u32[]{:S(2)}) %copy-start.3) | copy-done | bytes 1179672
  1.3 0.7 copy-done.4
  2.6 1.0 copy-done.5
  3.6 6.0 %collective-permute-start = (f32[400,384]{1,0:T(8,128)S(1)}, f32[400,384]{1,0:T(8,128)S(1)}, u32[]{:S(2)}, u32[]{:S(2)}) collective-permute-start(f32[400,384]{1,0:T(8,128)S(1)} %get-tuple-element.32), channel_id=1, source_target_pairs={{0,1},{1,2},{2,3},{3,4},{4,5},{5,6},{6,7},{7,8},{8,9},{9,10},{10,1... | collective-permute-start | bytes 1843208 | tf_op jit(solution)/shard_map/ppermute | solution.py:20
  9.7 4.7 %collective-permute-start.1 = (f32[400,384]{1,0:T(8,128)S(1)}, f32[400,384]{1,0:T(8,128)S(1)}, u32[]{:S(2)}, u32[]{:S(2)}) collective-permute-start(f32[400,384]{1,0:T(8,128)S(1)} %get-tuple-element.33), channel_id=1, source_target_pairs={{0,511},{1,0},{2,1},{3,2},{4,3},{5,4},{6,5},{7,6},{8,7},{9,8},{10,... | collective-permute-start | bytes 1843208 | tf_op jit(solution)/shard_map/ppermute | solution.py:20
  14.3 1.9 %collective-permute-start.2 = (f32[64,640]{1,0:T(8,128)S(1)}, f32[64,640]{1,0:T(8,128)S(1)}, u32[]{:S(2)}, u32[]{:S(2)}) collective-permute-start(f32[64,640]{1,0:T(8,128)S(1)} %get-tuple-element.34), channel_id=1, source_target_pairs={{0,2},{1,3},{2,4},{3,5},{4,6},{5,7},{6,8},{7,9},{8,10},{9,11},{10,... | collective-permute-start | bytes 491528 | tf_op jit(solution)/shard_map/ppermute | solution.py:20
  16.3 10.4 %collective-permute-start.3 = (f32[64,640]{1,0:T(8,128)S(1)}, f32[64,640]{1,0:T(8,128)S(1)}, u32[]{:S(2)}, u32[]{:S(2)}) collective-permute-start(f32[64,640]{1,0:T(8,128)S(1)} %get-tuple-element.35), channel_id=1, source_target_pairs={{0,510},{1,511},{2,0},{3,1},{4,2},{5,3},{6,4},{7,5},{8,6},{9,7},{1... | collective-permute-start | bytes 491528 | tf_op jit(solution)/shard_map/ppermute | solution.py:20
  26.7 19.3 %all_to_all.10.in_ref = f32[32,1,128]{2,1,0:T(1,128)S(1)} all-to-all(f32[32,1,128]{2,1,0:T(1,128)S(1)} %get-tuple-element.29), channel_id=1, replica_groups=mesh['blk'=16,'rep'=32] {'rep'}, dimensions={0} | all-to-all | bytes 32768 | tf_op jit(solution)/shard_map/all_to_all | solution.py:294
  45.9 0.8 row_sum.1
  46.7 5.3 %all-to-all-start.1 = ((f32[16,1,128]{2,1,0:T(1,128)}), f32[16,1,128]{2,1,0:T(1,128)S(1)}, u32[]{:S(2)}, u32[]{:S(2)}) async-start(f32[16,1,128]{2,1,0:T(1,128)} %row_sum.1), calls=%async_computation.1 | async-start | bytes 16384 | tf_op jit(solution)/shard_map/all_to_all | solution.py:296
  52.7 0.8 copy-done.7
  53.5 0.8 copy-done.9
  54.4 1.3 %copy-done.6 = f32[384,768]{1,0:T(8,128)S(1)} copy-done((f32[384,768]{1,0:T(8,128)S(1)}, f32[384,768]{1,0:T(8,128)}, u32[]{:S(2)}) %copy-start.6) | copy-done | bytes 1179672
  55.6 1.1 %copy-done.8 = f32[400,384]{1,0:T(8,128)S(1)} copy-done((f32[400,384]{1,0:T(8,128)S(1)}, f32[400,384]{1,0:T(8,128)}, u32[]{:S(2)}) %copy-start.8) | copy-done | bytes 614424
  56.7 1.1 %copy-done.10 = f32[400,384]{1,0:T(8,128)S(1)} copy-done((f32[400,384]{1,0:T(8,128)S(1)}, f32[400,384]{1,0:T(8,128)}, u32[]{:S(2)}) %copy-start.10) | copy-done | bytes 614424
  57.8 0.9 copy-done.12
  58.7 15.1 %first_iteration.1 = (f32[384,1024]{1,0:T(8,128)}, f32[320,640]{1,0:T(8,128)S(1)}, f32[320,640]{1,0:T(8,128)S(1)}, f32[384,1024]{1,0:T(8,128)}, f32[320,640]{1,0...) custom-call(f32[384,768]{1,0:T(8,128)S(1)} %copy-done.6, ...), custom_call_target="tpu_custom_call" | custom-call | flops 10000000000 | bytes 1048576 | tf_op jit(solution)/shard_map/first_iteration/pallas_call | solution.py:268
  73.8 6.2 %second_square.1 = (f32[384,1024]{1,0:T(8,128)}, bf16[1024,1024]{1,0:T(8,128)(2,1)}, bf16[1024,1024]{1,0:T(8,128)(2,1)}, f32[384,512]{1,0:T(8,128)S(1)}, f32[800...) custom-call(f32[16,1,128]{2,1,0:T(1,128)S(1)} %all-to-all-done.1.refs_0_, ...), custom_call_target="tpu_custom_call" | custom-call | flops 1000000000 | bytes 1048576 | tf_op jit(solution)/shard_map/second_square/pallas_call | solution.py:268
  79.9 3.7 %collective-permute-start.4 = (f32[800,128]{1,0:T(8,128)S(1)}, f32[800,128]{1,0:T(8,128)S(1)}, u32[]{:S(2)}, u32[]{:S(2)}) collective-permute-start(f32[800,128]{1,0:T(8,128)S(1)} %get-tuple-element.51), channel_id=1, source_target_pairs={{0,1},{1,2},{2,3},{3,4},{4,5},{5,6},{6,7},{7,8},{8,9},{9,10},{10,1... | collective-permute-start | bytes 1228808 | tf_op jit(solution)/shard_map/ppermute | solution.py:20
  83.6 1.9 %collective-permute-start.5 = (f32[800,128]{1,0:T(8,128)S(1)}, f32[800,128]{1,0:T(8,128)S(1)}, u32[]{:S(2)}, u32[]{:S(2)}) collective-permute-start(f32[800,128]{1,0:T(8,128)S(1)} %get-tuple-element.52), channel_id=1, source_target_pairs={{0,511},{1,0},{2,1},{3,2},{4,3},{5,4},{6,5},{7,6},{8,7},{9,8},{10,... | collective-permute-start | bytes 1228808 | tf_op jit(solution)/shard_map/ppermute | solution.py:20
  85.6 1.6 %copy-done = bf16[1024,1024]{1,0:T(8,128)(2,1)S(1)} copy-done((bf16[1024,1024]{1,0:T(8,128)(2,1)S(1)}, bf16[1024,1024]{1,0:T(8,128)(2,1)}, u32[]{:S(2)}) %copy-start) | copy-done | bytes 2097176
  87.2 7.0 %second_cubic.1.part_ref = f32[384,1024]{1,0:T(8,128)S(1)} custom-call(bf16[1024,1024]{1,0:T(8,128)(2,1)S(1)} %copy-done, bf16[1024,1024]{1,0:T(8,128)(2,1)} %get-tuple-element.45.xl, f32[384,512]{1,0:T(8,128)S(1)} %get-tuple-element.46.s2_ref, f32[8,1024]{1,0:T(8,128)S(1)} %get-tuple-element.43.refs_8_.ko_ref, f32[8,640]{1,0:T(8,128)S(1)} %get-tuple-element.47.kl_ref, ...), custom_call_target="tpu_custom_call" | custom-call | flops 10000000000 | bytes 1048576 | tf_op jit(solution)/shard_map/second_cubic/pallas_call | solution.py:268
  94.2 4.6 %collective-permute-done.5.fr_ref = f32[800,128]{1,0:T(8,128)S(1)} collective-permute-done((f32[800,128]{1,0:T(8,128)S(1)}, f32[800,128]{1,0:T(8,128)S(1)}, u32[]{:S(2)}, u32[]{:S(2)}) %collective-permute-start.5) | collective-permute-done | bytes 409632 | tf_op jit(solution)/shard_map/ppermute | solution.py:20
  98.8 4.1 %result.1 = f32[384,768]{1,0:T(8,128)} custom-call(f32[384,1024]{1,0:T(8,128)S(1)} %second_cubic.1.part_ref, f32[384,1024]{1,0:T(8,128)S(1)} %copy-done.2, bf16[1024,1024]{1,0:T(8,128)(2,1)S(1)} %copy-done.1, bf16[1024,1024]{1,0:T(8,128)(2,1)} %get-tuple-element.45.xl, f32[8,1024]{1,0:T(8,128)S(1)} %get-tuple-element.43.refs_8_.ko_ref, ...), custom_call_target="tpu_custom_call" | custom-call | flops 1000000000 | bytes 1048576 | tf_op jit(solution)/shard_map/result/pallas_call | solution.py:268
  (23 shorter events, 1.3 us)
Async XLA Ops:
  0.0 1.3 %copy-start.3 = (f32[6,64,768]{2,1,0:T(8,128)S(1)}, f32[6,64,768]{2,1,0:T(8,128)}, u32[]{:S(2)}) copy-start(f32[6,64,768]{2,1,0:T(8,128)} %param.2) | copy-start | bytes 3538948
  1.3 0.7 copy-start.4
  2.6 1.0 copy-start.5
  3.6 49.1 %collective-permute-start = (f32[400,384]{1,0:T(8,128)S(1)}, f32[400,384]{1,0:T(8,128)S(1)}, u32[]{:S(2)}, u32[]{:S(2)}) collective-permute-start(f32[400,384]{1,0:T(8,128)S(1)} %get-tuple-element.32), channel_id=1, source_target_pairs={{0,1},{1,2},{2,3},{3,4},{4,5},{5,6},{6,7},{7,8},{8,9},{9,10},{10,1... | collective-permute-start | bytes 1843208 | tf_op jit(solution)/shard_map/ppermute | solution.py:20
  9.7 43.9 %collective-permute-start.1 = (f32[400,384]{1,0:T(8,128)S(1)}, f32[400,384]{1,0:T(8,128)S(1)}, u32[]{:S(2)}, u32[]{:S(2)}) collective-permute-start(f32[400,384]{1,0:T(8,128)S(1)} %get-tuple-element.33), channel_id=1, source_target_pairs={{0,511},{1,0},{2,1},{3,2},{4,3},{5,4},{6,5},{7,6},{8,7},{9,8},{10,... | collective-permute-start | bytes 1843208 | tf_op jit(solution)/shard_map/ppermute | solution.py:20
  14.3 37.7 %collective-permute-start.2 = (f32[64,640]{1,0:T(8,128)S(1)}, f32[64,640]{1,0:T(8,128)S(1)}, u32[]{:S(2)}, u32[]{:S(2)}) collective-permute-start(f32[64,640]{1,0:T(8,128)S(1)} %get-tuple-element.34), channel_id=1, source_target_pairs={{0,2},{1,3},{2,4},{3,5},{4,6},{5,7},{6,8},{7,9},{8,10},{9,11},{10,... | collective-permute-start | bytes 491528 | tf_op jit(solution)/shard_map/ppermute | solution.py:20
  16.3 35.7 %collective-permute-start.3 = (f32[64,640]{1,0:T(8,128)S(1)}, f32[64,640]{1,0:T(8,128)S(1)}, u32[]{:S(2)}, u32[]{:S(2)}) collective-permute-start(f32[64,640]{1,0:T(8,128)S(1)} %get-tuple-element.35), channel_id=1, source_target_pairs={{0,510},{1,511},{2,0},{3,1},{4,2},{5,3},{6,4},{7,5},{8,6},{9,7},{1... | collective-permute-start | bytes 491528 | tf_op jit(solution)/shard_map/ppermute | solution.py:20
  46.7 27.0 %all-to-all-start.1 = ((f32[16,1,128]{2,1,0:T(1,128)}), f32[16,1,128]{2,1,0:T(1,128)S(1)}, u32[]{:S(2)}, u32[]{:S(2)}) async-start(f32[16,1,128]{2,1,0:T(1,128)} %row_sum.1), calls=%async_computation.1 | async-start | bytes 16384 | tf_op jit(solution)/shard_map/all_to_all | solution.py:296
  52.0 0.7 copy-start.11
  52.7 0.8 copy-start.7
  53.5 0.8 copy-start.9
  54.4 1.3 %copy-start.6 = (f32[384,768]{1,0:T(8,128)S(1)}, f32[384,768]{1,0:T(8,128)}, u32[]{:S(2)}) copy-start(f32[384,768]{1,0:T(8,128)} %copy-done.5) | copy-start | bytes 3538948
  55.6 1.1 %copy-start.8 = (f32[400,384]{1,0:T(8,128)S(1)}, f32[400,384]{1,0:T(8,128)}, u32[]{:S(2)}) copy-start(f32[400,384]{1,0:T(8,128)} %copy-done.7) | copy-start | bytes 1843204
  56.7 1.1 %copy-start.10 = (f32[400,384]{1,0:T(8,128)S(1)}, f32[400,384]{1,0:T(8,128)}, u32[]{:S(2)}) copy-start(f32[400,384]{1,0:T(8,128)} %copy-done.9) | copy-start | bytes 1843204
  57.8 0.9 copy-start.12
  79.9 14.2 %collective-permute-start.4 = (f32[800,128]{1,0:T(8,128)S(1)}, f32[800,128]{1,0:T(8,128)S(1)}, u32[]{:S(2)}, u32[]{:S(2)}) collective-permute-start(f32[800,128]{1,0:T(8,128)S(1)} %get-tuple-element.51), channel_id=1, source_target_pairs={{0,1},{1,2},{2,3},{3,4},{4,5},{5,6},{6,7},{7,8},{8,9},{9,10},{10,1... | collective-permute-start | bytes 1228808 | tf_op jit(solution)/shard_map/ppermute | solution.py:20
  83.6 15.2 %collective-permute-start.5 = (f32[800,128]{1,0:T(8,128)S(1)}, f32[800,128]{1,0:T(8,128)S(1)}, u32[]{:S(2)}, u32[]{:S(2)}) collective-permute-start(f32[800,128]{1,0:T(8,128)S(1)} %get-tuple-element.52), channel_id=1, source_target_pairs={{0,511},{1,0},{2,1},{3,2},{4,3},{5,4},{6,5},{7,6},{8,7},{9,8},{10,... | collective-permute-start | bytes 1228808 | tf_op jit(solution)/shard_map/ppermute | solution.py:20
  85.6 1.6 %copy-start = (bf16[1024,1024]{1,0:T(8,128)(2,1)S(1)}, bf16[1024,1024]{1,0:T(8,128)(2,1)}, u32[]{:S(2)}) copy-start(bf16[1024,1024]{1,0:T(8,128)(2,1)} %get-tuple-element.44.xh) | copy-start | bytes 6291460
  87.2 11.6 %copy-start.1 = (bf16[1024,1024]{1,0:T(8,128)(2,1)S(1)}, bf16[1024,1024]{1,0:T(8,128)(2,1)}, u32[]{:S(2)}) copy-start(bf16[1024,1024]{1,0:T(8,128)(2,1)} %get-tuple-element.44.xh) | copy-start | bytes 6291460
  87.2 11.6 %copy-start.2 = (f32[384,1024]{1,0:T(8,128)S(1)}, f32[384,1024]{1,0:T(8,128)}, u32[]{:S(2)}) copy-start(f32[384,1024]{1,0:T(8,128)} %get-tuple-element.49.x_ref) | copy-start | bytes 4718596

commit v2 on v0

v2 whole, which is shorter than its diff:
```python
import math

import jax
import jax.numpy as jnp
from jax import lax
from jax.experimental import pallas as pl
from jax.experimental.pallas import tpu as pltpu
from jax.sharding import PartitionSpec as P

BS = 64
AXES = ("blk", "rep")
F32 = jnp.float32
BF16 = jnp.bfloat16
VMEM = pl.BlockSpec(memory_space=pltpu.VMEM)
HBM = pl.BlockSpec(memory_space=pltpu.HBM)


def across(block):
    n = lax.axis_size(AXES)
    return lax.ppermute(block, AXES, [(i, (i + 1 if i % 2 else i - 1) % n) for i in range(n)])


def inside(block):
    n = lax.axis_size(AXES)
    return lax.ppermute(block, AXES, [(i, i ^ 1) for i in range(n)])


def odd():
    return lax.rem(lax.axis_index("rep"), 2) == 1


def zeros(rows, blocks):
    return jnp.zeros((rows, blocks * BS), F32)


def lanes(*parts):
    return jnp.concatenate([p for p in parts if p.shape[1]], axis=1)


def stack(*parts):
    return jnp.concatenate(parts, axis=0)


def split(x):
    high = x.astype(BF16)
    return high, (x - high.astype(F32)).astype(BF16)


def dot(a, b):
    return lax.dot_general(a, b, (((1,), (0,)), ((), ())), preferred_element_type=F32)


def dot3(a_high, a_low, b_high, b_low):
    return dot(a_high, b_high) + (dot(a_high, b_low) + dot(a_low, b_high))


def store(pair, start, value):
    for ref, part in zip(pair, split(value)):
        ref[start : start + value.shape[0], :] = part


def masked_rows(x, mask):
    return stack(*[x[BS * i : BS * (i + 1)] * mask[i : i + 1] for i in range(x.shape[0] // BS)])


def own_product(left, right):
    out = []
    for p in range(3):
        rows, reach = slice(128 * p, 128 * p + 128), slice(128 * p, 128 * p + 768)
        part = dot3(left[0][rows, reach], left[1][rows, reach], right[0][reach, reach], right[1][reach, reach])
        out.append(lanes(zeros(128, 2 * p), part, zeros(128, 4 - 2 * p)))
    return stack(*out)


def own_window(x):
    n = x.shape[0] // 6 if x.shape[0] > 8 else 1
    out = [lanes(x[0:n, BS:], zeros(n, 5))]
    for i in range(1, 6):
        out.append(lanes(zeros(n, i - 1), x[n * i : n * (i + 1)], zeros(n, 5 - i)))
    return stack(*out)


def mirror(a, lower):
    br = lax.broadcasted_iota(jnp.int32, a.shape, 0) // BS
    bc = lax.broadcasted_iota(jnp.int32, a.shape, 1) // BS
    keep = br >= bc if lower else br <= bc
    return jnp.where(keep, a, a.T)


def prepare_kernel(h_hbm, pat_hbm, m_ref, mask_ref, b_ref, a_ref, ssq_hbm, h_ref, pat_ref, ssq_ref, sem):
    fetch_pat = pltpu.make_async_copy(pat_hbm, pat_ref, sem.at[0])
    fetch_h = pltpu.make_async_copy(h_hbm, h_ref, sem.at[1])
    fetch_h.start()
    fetch_pat.start()
    fetch_pat.wait()
    pat = pat_ref[...].astype(F32)
    owner = lax.broadcasted_iota(jnp.int32, (12, 12 * BS), 1) // BS
    spread = (owner == lax.broadcasted_iota(jnp.int32, (12, 12 * BS), 0)).astype(F32)
    mask = stack(dot(pat, spread), jnp.zeros((2, 12 * BS), F32))
    mask_ref[...] = mask
    side = odd()
    for start, part in ((320, mask[:, 64:448]), (328, lanes(mask[:, 448:768], zeros(8, 1)))):
        b_ref[start : start + 8, :] = part
        a_ref[start : start + 8, :] = part
    fetch_h.wait()
    total = jnp.zeros((8, 128), F32)
    rows = []
    for i in range(6):
        at = slice(BS * i, BS * (i + 1))
        row = h_ref[at, :] * mask[i : i + 1, :]
        m_ref[at, :] = row
        square = row * row
        for a in range(8):
            for b in range(6):
                total = total + square[8 * a : 8 * a + 8, 128 * b : 128 * b + 128]
        rows.append(row)
    ssq_ref[...] = jnp.zeros(ssq_ref.shape, F32) + jnp.sum(total)
    send_ssq = pltpu.make_async_copy(ssq_ref, ssq_hbm, sem.at[0])
    send_ssq.start()
    for i in range(5):
        at = slice(BS * i, BS * (i + 1))
        to_right, to_left = rows[i + 1][:, 64:448], rows[i][:, 384:768]
        b_ref[at, :] = jnp.where(side, to_right, to_left)
        a_ref[at, :] = jnp.where(side, to_left, to_right)
    send_ssq.wait()


def fetch(sem, *pairs):
    copies = [pltpu.make_async_copy(source, target, sem.at[i]) for i, (source, target) in enumerate(pairs)]
    for copy in copies:
        copy.start()
    return copies


def halos(across_ref, inside_ref):
    side = odd()
    fb, fa = across_ref[...], inside_ref[...]
    return jnp.where(side, fa, fb), jnp.where(side, fb, fa)


def surroundings(own, fl, fr, g):
    fl, fr = fl[0:320] * g, fr[0:320] * g
    low = stack(*[lanes(zeros(BS, i), fl[BS * i : BS * (i + 1)], zeros(BS, 4 - i)) for i in range(5)])
    high = stack(*[lanes(zeros(BS, i), fr[BS * i : BS * (i + 1)], zeros(BS, 4 - i)) for i in range(5)])
    cross_l = own[:, 0:384].T[0:320]
    cross_r = own[:, 640:1024].T[64:384]
    hl = lanes(zeros(320, 1), low[:, 0:320], mirror(low[:, 320:640], True), cross_l[:, 0:320])
    hr = lanes(cross_r[:, 64:384], mirror(high[:, 0:320], False), high[:, 320:640], zeros(320, 1))
    return hl, hr


def masks(mask_own, fl, fr):
    mask_l, mask_r = [], []
    for i in range(5):
        band = lanes(fl[321 + i : 322 + i], fl[329 + i : 330 + i, 0:320])
        mask_l.append(lanes(zeros(1, 1 + i), band, zeros(1, 4 - i))[:, 384:1024])
        band = lanes(fr[320 + i : 321 + i], fr[328 + i : 329 + i, 0:320])
        mask_r.append(lanes(zeros(1, i), band, zeros(1, 5 - i))[:, 0:640])
    return mask_own if mask_own is None else own_window(mask_own), stack(*mask_l), stack(*mask_r)


def square_kernel(m_ref, mask_ref, b_hbm, a_hbm, s_ref, top_ref, oh, ol, wh, wl, b_ref, a_ref, sem):
    copies = fetch(sem, (b_hbm, b_ref), (a_hbm, a_ref))
    m = m_ref[...]
    own = own_window(m)
    for copy in copies:
        copy.wait()
    fl, fr = halos(b_ref, a_ref)
    top = jnp.maximum(jnp.max(jnp.abs(fl[0:320])), jnp.max(jnp.abs(fr[0:320])))
    top = jnp.maximum(jnp.maximum(top, jnp.max(jnp.abs(m))), 1e-11)
    top_ref[...] = jnp.zeros(top_ref.shape, F32) + top
    own = own * (1.0 / top)
    hl, hr = surroundings(own, fl, fr, 1.0 / top)
    store((oh, ol), 0, own)
    store((wh, wl), 0, lanes(hl[:, 384:1024], zeros(320, 6)))
    store((wh, wl), 320, own)
    store((wh, wl), 704, lanes(zeros(320, 6), hr[:, 0:640]))
    s_ref[...] = masked_rows(own_product((oh, ol), (wh, wl)), own_window(mask_ref[...]))


def send_kernel(ssq_ref, s_ref, top_ref, b_ref, a_ref, new_top_ref, out_hbm, out_ref, sem):
    out_ref[...] = jnp.zeros(out_ref.shape, F32) + jnp.sum(ssq_ref[...]) / 128.0
    copy = pltpu.make_async_copy(out_ref, out_hbm, sem.at[0])
    copy.start()
    side = odd()
    new_top_ref[...] = top_ref[...]
    scale = zeros(BS, 3) + top_ref[0:1, 0:1]
    row = [s_ref[BS * i : BS * (i + 1), :] for i in range(6)]
    to_right = stack(
        lanes(row[1][:, 64:384], row[5][:, 320:384]),
        lanes(row[2][:, 128:384], row[4][:, 256:384]),
        lanes(row[3][:, 192:384], scale),
    )
    to_left = stack(
        lanes(row[4][:, 640:960], row[0][:, 640:704]),
        lanes(row[3][:, 640:896], row[1][:, 640:768]),
        lanes(row[2][:, 640:832], scale),
    )
    b_ref[...] = jnp.where(side, to_right, to_left)
    a_ref[...] = jnp.where(side, to_left, to_right)
    copy.wait()


def halo_square_kernel(top_ref, m_ref, b_hbm, a_hbm, sl_hbm, sr_hbm, b_ref, a_ref, sl_ref, sr_ref, sem):
    copies = fetch(sem, (b_hbm, b_ref), (a_hbm, a_ref))
    g = 1.0 / top_ref[0:1, 0:1]
    own = own_window(m_ref[...]) * g
    for copy in copies:
        copy.wait()
    fl, fr = halos(b_ref, a_ref)
    _, mask_l, mask_r = masks(None, fl, fr)
    hl, hr = surroundings(own, fl, fr, g)
    right = stack(zeros(64, 6), lanes(hl[:, 0:384].T[64:384], zeros(320, 1)), hl[:, 384:768], own[0:320, 0:384])
    s_l = dot3(*split(hl), *split(right))
    sl_ref[...] = masked_rows(s_l[:, 0:320], mask_l[:, 0:320])
    keep_l = pltpu.make_async_copy(sl_ref, sl_hbm, sem.at[0])
    keep_l.start()
    right = stack(own[64:384, 640:1024], hr[:, 256:640], lanes(zeros(320, 1), hr[:, 640:1024].T[0:320]), zeros(64, 6))
    s_r = dot3(*split(hr), *split(right))
    sr_ref[...] = masked_rows(s_r[:, 64:384], mask_r[:, 320:640])
    keep_r = pltpu.make_async_copy(sr_ref, sr_hbm, sem.at[1])
    keep_r.start()
    keep_l.wait()
    keep_r.wait()


def second_kernel(
    norms_ref, top_ref, m_ref, mask_ref, s_ref, b1_hbm, a1_hbm, sl_hbm, sr_hbm, b2_hbm, a2_hbm,
    x_ref, xh, xl, s2_ref, b_ref, a_ref, inv_ref, ko_ref, kl_ref, kr_ref,
    oh, ol, lh, ll, rh, rl, wh, wl, b1_ref, a1_ref, sl_ref, sr_ref, b2_ref, a2_ref, sem, *, size
):
    copies = fetch(
        sem, (b1_hbm, b1_ref), (a1_hbm, a1_ref), (sl_hbm, sl_ref), (sr_hbm, sr_ref), (b2_hbm, b2_ref), (a2_hbm, a2_ref)
    )
    top = top_ref[0:1, 0:1]
    own = own_window(m_ref[...]) * (1.0 / top)
    store((oh, ol), 0, own)
    s = s_ref[...]
    store((wh, wl), 320, s)
    for copy in copies:
        copy.wait()
    fl, fr = halos(b1_ref, a1_ref)
    mask_o, mask_l, mask_r = masks(mask_ref[...], fl, fr)
    ko_ref[...] = stack(mask_o, jnp.zeros((2, 1024), F32))
    kl_ref[...] = stack(mask_l, jnp.zeros((3, 640), F32))
    kr_ref[...] = stack(mask_r, jnp.zeros((3, 640), F32))
    hl, hr = surroundings(own, fl, fr, 1.0 / top)

    store((wh, wl), 0, lanes(sl_ref[...], s[:, 0:384].T[0:320, 0:320], zeros(320, 6)))
    store((wh, wl), 704, lanes(zeros(320, 6), s[:, 640:1024].T[64:384, 64:384], sr_ref[...]))
    t_o = masked_rows(own_product((oh, ol), (wh, wl)), mask_o)
    fl, fr = halos(b2_ref, a2_ref)
    far_l = stack(
        fl[0:64, 0:320],
        lanes(zeros(BS, 1), fl[64:128, 0:256]),
        lanes(zeros(BS, 2), fl[128:192, 0:192]),
        lanes(zeros(BS, 3), fl[64:128, 256:384]),
        lanes(zeros(BS, 4), fl[0:64, 320:384]),
    )
    far_r = stack(
        lanes(fr[0:64, 320:384], zeros(BS, 4)),
        lanes(fr[64:128, 256:384], zeros(BS, 3)),
        lanes(fr[128:192, 0:192], zeros(BS, 2)),
        lanes(fr[64:128, 0:256], zeros(BS, 1)),
        fr[0:64, 0:320],
    )
    ratio_l, ratio_r = fl[128:129, 192:193] / top, fr[128:129, 192:193] / top
    store((lh, ll), 0, zeros(64, 10))
    store((lh, ll), 64, lanes((far_l * ratio_l * ratio_l).T, zeros(320, 5)))
    lh[384:1024, :], ll[384:1024, :] = wh[0:640, 0:640], wl[0:640, 0:640]
    t_l = masked_rows(dot3(*split(hl), lh[...], ll[...]), mask_l)
    rh[0:640, :], rl[0:640, :] = wh[384:1024, 384:1024], wl[384:1024, 384:1024]
    store((rh, rl), 640, lanes(zeros(320, 5), (far_r * ratio_r * ratio_r).T))
    store((rh, rl), 960, zeros(64, 10))
    t_r = masked_rows(dot3(*split(hr), rh[...], rl[...]), mask_r)

    frob = jnp.sqrt(jnp.sum(norms_ref[...], keepdims=True)[0] / 128.0)
    inverse = 3.0 * frob / size
    inv_ref[...] = jnp.zeros(inv_ref.shape, F32) + inverse
    r = top / inverse
    c1 = 1.5 * r
    c3 = 0.5 * r * r * r
    x = c1 * own - c3 * t_o
    x_ref[...] = x
    store((xh, xl), 0, lanes(c1 * hl[:, 384:1024] - c3 * t_l, zeros(320, 6)))
    store((xh, xl), 320, x)
    store((xh, xl), 704, lanes(zeros(320, 6), c1 * hr[:, 0:640] - c3 * t_r))
    s2 = dot3(xh[320:704, :], xl[320:704, :], xh[:, 256:768], xl[:, 256:768])
    s2 = masked_rows(s2, mask_o[:, 256:768])
    s2_ref[...] = s2

    def pack(block):
        tail = lanes(block[0:160, 256:320], block[160:320, 256:320])
        return stack(block[:, 0:128], block[:, 128:256], tail)

    side = odd()
    to_right, to_left = pack(s2[64:384, 128:448]), pack(s2[0:320, 64:384])
    b_ref[...] = jnp.where(side, to_right, to_left)
    a_ref[...] = jnp.where(side, to_left, to_right)


def third_kernel(x_ref, xh, xl, s2_ref, ko_ref, kl_ref, kr_ref, inv_ref, out_ref, wh, wl):
    ah, al = xh[320:704, :], xl[320:704, :]
    s2_a = masked_rows(dot3(ah, al, xh[:, 0:256], xl[:, 0:256]), ko_ref[0:6, 0:256])
    s2_b = masked_rows(dot3(ah, al, xh[:, 768:1024], xl[:, 768:1024]), ko_ref[0:6, 768:1024])
    s2_l = dot3(xh[0:320, 0:640], xl[0:320, 0:640], xh[0:640, 256:640], xl[0:640, 256:640])
    s2_l = masked_rows(s2_l, kl_ref[0:5, 256:640])[:, 64:384]
    s2_r = dot3(xh[704:1024, 384:1024], xl[704:1024, 384:1024], xh[384:1024, 384:768], xl[384:1024, 384:768])
    s2_r = masked_rows(s2_r, kr_ref[0:5, 0:384])[:, 0:320]
    store((wh, wl), 0, lanes(zeros(320, 5), s2_l, zeros(320, 6)))
    store((wh, wl), 320, lanes(s2_a, s2_ref[...], s2_b))
    store((wh, wl), 704, lanes(zeros(320, 6), s2_r, zeros(320, 5)))
    left = (xh.at[320:704, :], xl.at[320:704, :])
    cubic = own_product(left, (wh, wl))
    inverse = inv_ref[0:1, 0:1]
    for i in range(6):
        at = slice(BS * i, BS * (i + 1))
        row = (1.5 * x_ref[at, :] - 0.5 * (cubic[at] * ko_ref[i : i + 1, :])) * inverse
        if i == 0:
            out_ref[at, :] = lanes(zeros(BS, 1), row[:, 0:704])
        else:
            out_ref[at, :] = row[:, 64 * (i - 1) : 64 * (i - 1) + 768]


def last_kernel(part_ref, xh, xl, ko_ref, inv_ref, fb_ref, fa_ref, out_hbm, out_ref, sem):
    side = odd()
    fb, fa = fb_ref[...], fa_ref[...]
    corner_l, corner_r = [
        lanes(f[0:320], f[320:640], stack(f[640:800, 0:64], f[640:800, 64:128]))
        for f in (jnp.where(side, fa, fb), jnp.where(side, fb, fa))
    ]
    half = 0.5 * inv_ref[0:1, 0:1]
    corner_l = stack(lanes(corner_l, zeros(320, 1)), zeros(64, 6))
    corner_r = stack(zeros(64, 6), lanes(zeros(320, 1), corner_r))
    add_l = dot3(xh[320:640, 0:384], xl[320:640, 0:384], *split(corner_l))
    add_r = dot3(xh[384:704, 640:1024], xl[384:704, 640:1024], *split(corner_r))
    copies = []
    for i in range(6):
        at = slice(BS * i, BS * (i + 1))
        parts = []
        if i < 5:
            part = add_l[at, 64 * i : 320] * (half * ko_ref[i : i + 1, 64 * i : 320])
            parts.append(lanes(zeros(BS, 1), part))
        parts.append(zeros(BS, 12 - (6 - i if i < 5 else 0) - i))
        if i > 0:
            part = add_r[BS * (i - 1) : BS * i, 64 : 64 + 64 * i]
            parts.append(part * (half * ko_ref[i : i + 1, 704 : 704 + 64 * i]))
        out_ref[at, :] = part_ref[at, :] - lanes(*parts)
        copies.append(pltpu.make_async_copy(out_ref.at[at, :], out_hbm.at[at, :], sem.at[i]))
        copies[-1].start()
    for copy in copies:
        copy.wait()


def call(kernel, outs, args, flops, name, mib, scratch=(), in_hbm=(), out_hbm=()):
    args = [pltpu.with_memory_space_constraint(a, pltpu.HBM) if i in in_hbm else a for i, a in enumerate(args)]
    return pl.pallas_call(
        kernel,
        out_shape=[(pltpu.HBM if i in out_hbm else pltpu.VMEM)(s, t) for i, (s, t) in enumerate(outs)],
        in_specs=[HBM if i in in_hbm else VMEM for i in range(len(args))],
        out_specs=[HBM if i in out_hbm else VMEM for i in range(len(outs))],
        scratch_shapes=list(scratch),
        compiler_params=pltpu.CompilerParams(vmem_limit_bytes=mib << 20),
        cost_estimate=pl.CostEstimate(flops=flops, bytes_accessed=1 << 20, transcendentals=0),
        name=name,
    )(*args)


def local(hamiltonian, pattern):
    n_blk, n_rep = lax.axis_size("blk"), lax.axis_size("rep")
    size = math.sqrt(n_blk * n_rep * 6 * BS)
    band = hamiltonian.reshape(6 * BS, 12 * BS)
    own, corner, mask_o, mask_h, scalar = ((384, 1024), F32), ((320, 320), F32), ((8, 1024), F32), ((8, 640), F32), ((8, 128), F32)
    dma = pltpu.SemaphoreType.DMA((2,))
    wide, tall = pltpu.VMEM((1024, 1024), BF16), pltpu.VMEM((1024, 640), BF16)
    rows, far = pltpu.VMEM((384, 1024), BF16), pltpu.VMEM((336, 384), F32)

    m, mask, to_b, to_a, ssq = call(
        prepare_kernel,
        [((384, 768), F32), ((8, 768), F32), ((336, 384), F32), ((336, 384), F32), ((n_rep, 1, 128), F32)],
        (band, pattern), 10**7, "prepare", 16,
        scratch=[pltpu.VMEM((384, 768), F32), pltpu.VMEM((6, 12), jnp.int32), pltpu.VMEM((n_rep, 1, 128), F32), dma],
        in_hbm=(0, 1), out_hbm=(4,),
    )
    first_b, first_a = across(to_b), inside(to_a)
    ssq = lax.all_to_all(ssq, "rep", 0, 0)
    s, top = call(
        square_kernel, [own, scalar], (m, mask, first_b, first_a), 10**9, "first_square", 24,
        scratch=[rows, rows, wide, wide, far, far, dma], in_hbm=(2, 3),
    )
    to_b, to_a, top, ssq = call(
        send_kernel, [((192, 384), F32), ((192, 384), F32), scalar, ((n_blk, 1, 128), F32)],
        (ssq, s, top), 10**6, "send", 16, scratch=[pltpu.VMEM((n_blk, 1, 128), F32), dma], out_hbm=(3,),
    )
    from_b, from_a = across(to_b), inside(to_a)
    ssq = lax.all_to_all(ssq, "blk", 0, 0)
    s_l, s_r = call(
        halo_square_kernel, [corner, corner], (top, m, first_b, first_a), 10**9, "halo_square", 24,
        scratch=[far, far, pltpu.VMEM(*corner), pltpu.VMEM(*corner), dma], in_hbm=(2, 3), out_hbm=(0, 1),
    )
    x, xh, xl, s2, to_b, to_a, inverse, ko, kl, kr = call(
        lambda *refs: second_kernel(*refs, size=size),
        [own, ((1024, 1024), BF16), ((1024, 1024), BF16), ((384, 512), F32),
         ((800, 128), F32), ((800, 128), F32), scalar, mask_o, mask_h, mask_h],
        (ssq, top, m, mask, s, first_b, first_a, s_l, s_r, from_b, from_a), 10**10, "second_square", 32,
        scratch=[rows] * 2 + [tall] * 4 + [wide] * 2 + [far] * 2 + [pltpu.VMEM(*corner)] * 2
        + [pltpu.VMEM((192, 384), F32)] * 2 + [pltpu.SemaphoreType.DMA((6,))], in_hbm=(5, 6, 7, 8, 9, 10),
    )
    from_b, from_a = across(to_b), inside(to_a)
    (part,) = call(
        third_kernel, [((384, 768), F32)], (x, xh, xl, s2, ko, kl, kr, inverse), 5 * 10**9, "second_cubic", 24,
        scratch=[wide] * 2,
    )
    (out,) = call(
        last_kernel, [((384, 768), F32)], (part, xh, xl, ko, inverse, from_b, from_a), 10**9, "result", 16,
        scratch=[pltpu.VMEM((384, 768), F32), pltpu.SemaphoreType.DMA((6,))], out_hbm=(0,),
    )
    return out.reshape(6, BS, 12 * BS)


def solution(mesh):
    placed = (P(AXES, None, None), P(AXES, None))
    return jax.shard_map(
        local, mesh=mesh, in_specs=placed, out_specs=P(AXES, None, None), check_vma=False
    )
```

time: 560 us -> 83.1 us (0.15)
  the two profiles are of different devices: /device:TPU:195 before, /device:TPU:2 now
where the time goes in v2:
time: 83.1 us; the launch traced here: 82.7 us
  starting transfers between devices  39.8 us (48%)
  Pallas kernels  30.1 us (36%)
  waiting for transfers between devices  11.5 us (14%)
  local copies, waits for them, and re-layouts  0.95 us (1%)
    pallas_call x7, Pallas kernels, call(): pl.pallas_call(kernel, out_shape=[(pltpu.HBM if i in out_hbm else pltpu.V...  30.1 us
    ppermute x3, starting transfers between devices, across(): lax.ppermute(block, AXES, [(i, (i + 1 if i % 2 else i - 1) % n) for i in...  18.5 us
    all_to_all x1, starting transfers between devices, local(): ssq = lax.all_to_all(ssq, 'blk', 0, 0)  10 us
    ppermute x3, waiting for transfers between devices, across(): lax.ppermute(block, AXES, [(i, (i + 1 if i % 2 else i - 1) % n) for i in...  6.76 us
    ppermute x3, starting transfers between devices, inside(): return lax.ppermute(block, AXES, [(i, i ^ 1) for i in range(n)])  5.98 us
    all_to_all x1, starting transfers between devices, local(): ssq = lax.all_to_all(ssq, 'rep', 0, 0)  5.28 us
    all_to_all x1, waiting for transfers between devices, local(): ssq = lax.all_to_all(ssq, 'rep', 0, 0)  2.76 us
    all_to_all x1, waiting for transfers between devices, local(): ssq = lax.all_to_all(ssq, 'blk', 0, 0)  1.96 us
  transfers between devices with their start and end apart: 8, of which 4 were waited for; matrix products, arithmetic and copies ran while one was open for 0% of the time, Pallas kernels for 17%

profile of v2, /device:TPU:2, one launch (start us, length us, event | category | flops | bytes accessed | tf_op | source)
XLA Modules:
  0.0 82.7 jit_solution(15644120714877133682)
XLA Ops:
  0.0 2.6 %prepare.1 = (f32[384,768]{1,0:T(8,128)S(1)}, f32[8,768]{1,0:T(8,128)S(1)}, f32[336,384]{1,0:T(8,128)S(1)}, f32[336,384]{1,0:T(8,128)S(1)}, f32[32,1,128]{2,1,0:T(1,128)}) custom-call(f32[384,768]{1,0:T(8,128)} %bitcast.2, s32[6,12]{1,0:T(8,128)} %pat_hbm.1), custom_call_target="tpu_custom_call" | custom-call | flops 10000000 | bytes 1048576 | tf_op jit(solution)/shard_map/prepare/pallas_call | solution.py:357
  2.6 11.3 %collective-permute-start = (f32[336,384]{1,0:T(8,128)S(1)}, f32[336,384]{1,0:T(8,128)S(1)}, u32[]{:S(2)}, u32[]{:S(2)}) collective-permute-start(f32[336,384]{1,0:T(8,128)S(1)} %get-tuple-element.31), channel_id=1, source_target_pairs={{0,511},{1,2},{2,1},{3,4},{4,3},{5,6},{6,5},{7,8},{8,7},{9,10},{10... | collective-permute-start | bytes 1548296 | tf_op jit(solution)/shard_map/ppermute | solution.py:20
  14.0 1.9 %collective-permute-start.1 = (f32[336,384]{1,0:T(8,128)S(1)}, f32[336,384]{1,0:T(8,128)S(1)}, u32[]{:S(2)}, u32[]{:S(2)}) collective-permute-start(f32[336,384]{1,0:T(8,128)S(1)} %get-tuple-element.32), channel_id=1, source_target_pairs={{0,1},{1,0},{2,3},{3,2},{4,5},{5,4},{6,7},{7,6},{8,9},{9,8},{10,11... | collective-permute-start | bytes 1548296 | tf_op jit(solution)/shard_map/ppermute | solution.py:25
  15.9 5.3 %all-to-all-start = ((f32[32,1,128]{2,1,0:T(1,128)}), f32[32,1,128]{2,1,0:T(1,128)S(1)}, u32[]{:S(2)}, u32[]{:S(2)}) async-start(f32[32,1,128]{2,1,0:T(1,128)} %get-tuple-element.28), calls=%async_computation | async-start | bytes 32768 | tf_op jit(solution)/shard_map/all_to_all | solution.py:386
  21.2 1.8 %collective-permute-done.b_hbm.refs_5_ = f32[336,384]{1,0:T(8,128)S(1)} collective-permute-done((f32[336,384]{1,0:T(8,128)S(1)}, f32[336,384]{1,0:T(8,128)S(1)}, u32[]{:S(2)}, u32[]{:S(2)}) %collective-permute-start) | collective-permute-done | bytes 516128 | tf_op jit(solution)/shard_map/ppermute | solution.py:20
  22.9 0.0 collective-permute-done.1.a_hbm.refs_6_
  23.0 0.8 copy-done.1
  23.8 0.1 copy-done
  23.9 4.3 %first_square.1 = (f32[384,1024]{1,0:T(8,128)S(1)}, f32[8,128]{1,0:T(8,128)S(1)}) custom-call(f32[384,768]{1,0:T(8,128)S(1)} %get-tuple-element.29.m_ref.refs_2_, f32[8,768]{1,0:T(8,128)S(1)} %get-tuple-element.30.mask_ref.refs_3_, f32[336,384]{1,0:T(8,128)} %copy-done, f32[336,384]{1,0:T(8,128)} %copy-done.1), custom_call_target="tpu_custom_call" | custom-call | flops 1000000000 | bytes 1048576 | tf_op jit(solution)/shard_map/first_square/pallas_call | solution.py:357
  28.2 2.8 %all-to-all-done.ssq_ref = f32[32,1,128]{2,1,0:T(1,128)S(1)} async-done(((f32[32,1,128]{2,1,0:T(1,128)}), f32[32,1,128]{2,1,0:T(1,128)S(1)}, u32[]{:S(2)}, u32[]{:S(2)}) %all-to-all-start) | async-done | bytes 16416 | tf_op jit(solution)/shard_map/all_to_all | solution.py:386
  30.9 0.8 send.1
  31.7 4.7 %collective-permute-start.2 = (f32[192,384]{1,0:T(8,128)S(1)}, f32[192,384]{1,0:T(8,128)}, u32[]{:S(2)}, u32[]{:S(2)}) collective-permute-start(f32[192,384]{1,0:T(8,128)S(1)} %get-tuple-element.39), channel_id=1, source_target_pairs={{0,511},{1,2},{2,1},{3,4},{4,3},{5,6},{6,5},{7,8},{8,7},{9,10},{10... | collective-permute-start | bytes 884744 | tf_op jit(solution)/shard_map/ppermute | solution.py:20
  36.4 1.9 %collective-permute-start.3 = (f32[192,384]{1,0:T(8,128)S(1)}, f32[192,384]{1,0:T(8,128)}, u32[]{:S(2)}, u32[]{:S(2)}) collective-permute-start(f32[192,384]{1,0:T(8,128)S(1)} %get-tuple-element.40), channel_id=1, source_target_pairs={{0,1},{1,0},{2,3},{3,2},{4,5},{5,4},{6,7},{7,6},{8,9},{9,8},{10,11... | collective-permute-start | bytes 884744 | tf_op jit(solution)/shard_map/ppermute | solution.py:25
  38.3 10.0 %all-to-all-start.1 = ((f32[16,1,128]{2,1,0:T(1,128)}), f32[16,1,128]{2,1,0:T(1,128)S(1)}, u32[]{:S(2)}, u32[]{:S(2)}) async-start(f32[16,1,128]{2,1,0:T(1,128)} %get-tuple-element.35), calls=%async_computation.1 | async-start | bytes 16384 | tf_op jit(solution)/shard_map/all_to_all | solution.py:396
  48.3 5.2 %halo_square.1 = (f32[320,320]{1,0:T(8,128)}, f32[320,320]{1,0:T(8,128)}) custom-call(f32[8,128]{1,0:T(8,128)S(1)} %get-tuple-element.36.top_ref.refs_1_, f32[384,768]{1,0:T(8,128)S(1)} %get-tuple-element.29.m_ref.refs_2_, f32[336,384]{1,0:T(8,128)} %copy-done, f32[336,384]{1,0:T(8,128)} %copy-done.1), custom_call_target="tpu_custom_call" | custom-call | flops 1000000000 | bytes 1048576 | tf_op jit(solution)/shard_map/halo_square/pallas_call | solution.py:357
  53.5 2.0 %all-to-all-done.1.refs_0_ = f32[16,1,128]{2,1,0:T(1,128)S(1)} async-done(((f32[16,1,128]{2,1,0:T(1,128)}), f32[16,1,128]{2,1,0:T(1,128)S(1)}, u32[]{:S(2)}, u32[]{:S(2)}) %all-to-all-start.1) | async-done | bytes 8224 | tf_op jit(solution)/shard_map/all_to_all | solution.py:396
  55.5 0.0 collective-permute-done.3.refs_10_
  55.5 10.5 %second_square.1 = (f32[384,1024]{1,0:T(8,128)S(1)}, bf16[1024,1024]{1,0:T(8,128)(2,1)S(1)}, bf16[1024,1024]{1,0:T(8,128)(2,1)S(1)}, f32[384,512]{1,0:T(8,128)S(...) custom-call(f32[16,1,128]{2,1,0:T(1,128)S(1)} %all-to-all-done.1.ref, ...), custom_call_target="tpu_custom_call" | custom-call | flops 10000000000 | bytes 1048576 | tf_op jit(solution)/shard_map/second_square/pallas_call | solution.py:357
  66.0 2.5 %collective-permute-start.4 = (f32[800,128]{1,0:T(8,128)S(1)}, f32[800,128]{1,0:T(8,128)S(1)}, u32[]{:S(2)}, u32[]{:S(2)}) collective-permute-start(f32[800,128]{1,0:T(8,128)S(1)} %get-tuple-element.49), channel_id=1, source_target_pairs={{0,511},{1,2},{2,1},{3,4},{4,3},{5,6},{6,5},{7,8},{8,7},{9,10},{10... | collective-permute-start | bytes 1228808 | tf_op jit(solution)/shard_map/ppermute | solution.py:20
  68.5 2.1 %collective-permute-start.5 = (f32[800,128]{1,0:T(8,128)S(1)}, f32[800,128]{1,0:T(8,128)S(1)}, u32[]{:S(2)}, u32[]{:S(2)}) collective-permute-start(f32[800,128]{1,0:T(8,128)S(1)} %get-tuple-element.50), channel_id=1, source_target_pairs={{0,1},{1,0},{2,3},{3,2},{4,5},{5,4},{6,7},{7,6},{8,9},{9,8},{10,11... | collective-permute-start | bytes 1228808 | tf_op jit(solution)/shard_map/ppermute | solution.py:25
  70.7 4.7 %second_cubic.1.part_ref = f32[384,768]{1,0:T(8,128)S(1)} custom-call(f32[384,1024]{1,0:T(8,128)S(1)} %get-tuple-element.41.x_ref, bf16[1024,1024]{1,0:T(8,128)(2,1)S(1)} %get-tuple-element.42.xh, bf16[1024,1024]{1,0:T(8,128)(2,1)S(1)} %get-tuple-element.43.xl, f32[384,512]{1,0:T(8,128)S(1)} %get-tuple-element.44.s2_ref, ...), custom_call_target="tpu_custom_call" | custom-call | flops 5000000000 | bytes 1048576 | tf_op jit(solution)/shard_map/second_cubic/pallas_call | solution.py:357
  75.4 5.0 %collective-permute-done.4.fb_ref = f32[800,128]{1,0:T(8,128)S(1)} collective-permute-done((f32[800,128]{1,0:T(8,128)S(1)}, f32[800,128]{1,0:T(8,128)S(1)}, u32[]{:S(2)}, u32[]{:S(2)}) %collective-permute-start.4) | collective-permute-done | bytes 409632 | tf_op jit(solution)/shard_map/ppermute | solution.py:20
  80.4 0.0 collective-permute-done.5.fa_ref
  80.4 2.1 %result.1 = f32[384,768]{1,0:T(8,128)} custom-call(f32[384,768]{1,0:T(8,128)S(1)} %second_cubic.1.part_ref, bf16[1024,1024]{1,0:T(8,128)(2,1)S(1)} %get-tuple-element.42.xh, bf16[1024,1024]{1,0:T(8,128)(2,1)S(1)} %get-tuple-element.43.xl, f32[8,1024]{1,0:T(8,128)S(1)} %get-tuple-element.45.ko_ref, f32[8,128]{1,0:T(8,128)S(1)} %get-tuple-element.48.inv_ref, ...), custom_call_target="tpu_custom_call" | custom-call | flops 1000000000 | bytes 1048576 | tf_op jit(solution)/shard_map/result/pallas_call | solution.py:357
  (3 shorter events, 0.0 us)
Async XLA Ops:
  2.6 20.3 %collective-permute-start = (f32[336,384]{1,0:T(8,128)S(1)}, f32[336,384]{1,0:T(8,128)S(1)}, u32[]{:S(2)}, u32[]{:S(2)}) collective-permute-start(f32[336,384]{1,0:T(8,128)S(1)} %get-tuple-element.31), channel_id=1, source_target_pairs={{0,511},{1,2},{2,1},{3,4},{4,3},{5,6},{6,5},{7,8},{8,7},{9,10},{10... | collective-permute-start | bytes 1548296 | tf_op jit(solution)/shard_map/ppermute | solution.py:20
  14.0 9.0 %collective-permute-start.1 = (f32[336,384]{1,0:T(8,128)S(1)}, f32[336,384]{1,0:T(8,128)S(1)}, u32[]{:S(2)}, u32[]{:S(2)}) collective-permute-start(f32[336,384]{1,0:T(8,128)S(1)} %get-tuple-element.32), channel_id=1, source_target_pairs={{0,1},{1,0},{2,3},{3,2},{4,5},{5,4},{6,7},{7,6},{8,9},{9,8},{10,11... | collective-permute-start | bytes 1548296 | tf_op jit(solution)/shard_map/ppermute | solution.py:25
  15.9 15.0 %all-to-all-start = ((f32[32,1,128]{2,1,0:T(1,128)}), f32[32,1,128]{2,1,0:T(1,128)S(1)}, u32[]{:S(2)}, u32[]{:S(2)}) async-start(f32[32,1,128]{2,1,0:T(1,128)} %get-tuple-element.28), calls=%async_computation | async-start | bytes 32768 | tf_op jit(solution)/shard_map/all_to_all | solution.py:386
  22.9 1.0 %copy-start = (f32[336,384]{1,0:T(8,128)}, f32[336,384]{1,0:T(8,128)S(1)}, u32[]{:S(2)}) copy-start(f32[336,384]{1,0:T(8,128)S(1)} %collective-permute-done.b_hbm.refs_5_) | copy-start | bytes 1548292
  23.0 0.8 copy-start.1
  31.7 23.8 %collective-permute-start.2 = (f32[192,384]{1,0:T(8,128)S(1)}, f32[192,384]{1,0:T(8,128)}, u32[]{:S(2)}, u32[]{:S(2)}) collective-permute-start(f32[192,384]{1,0:T(8,128)S(1)} %get-tuple-element.39), channel_id=1, source_target_pairs={{0,511},{1,2},{2,1},{3,4},{4,3},{5,6},{6,5},{7,8},{8,7},{9,10},{10... | collective-permute-start | bytes 884744 | tf_op jit(solution)/shard_map/ppermute | solution.py:20
  36.4 19.1 %collective-permute-start.3 = (f32[192,384]{1,0:T(8,128)S(1)}, f32[192,384]{1,0:T(8,128)}, u32[]{:S(2)}, u32[]{:S(2)}) collective-permute-start(f32[192,384]{1,0:T(8,128)S(1)} %get-tuple-element.40), channel_id=1, source_target_pairs={{0,1},{1,0},{2,3},{3,2},{4,5},{5,4},{6,7},{7,6},{8,9},{9,8},{10,11... | collective-permute-start | bytes 884744 | tf_op jit(solution)/shard_map/ppermute | solution.py:25
  38.3 17.2 %all-to-all-start.1 = ((f32[16,1,128]{2,1,0:T(1,128)}), f32[16,1,128]{2,1,0:T(1,128)S(1)}, u32[]{:S(2)}, u32[]{:S(2)}) async-start(f32[16,1,128]{2,1,0:T(1,128)} %get-tuple-element.35), calls=%async_computation.1 | async-start | bytes 16384 | tf_op jit(solution)/shard_map/all_to_all | solution.py:396
  66.0 14.4 %collective-permute-start.4 = (f32[800,128]{1,0:T(8,128)S(1)}, f32[800,128]{1,0:T(8,128)S(1)}, u32[]{:S(2)}, u32[]{:S(2)}) collective-permute-start(f32[800,128]{1,0:T(8,128)S(1)} %get-tuple-element.49), channel_id=1, source_target_pairs={{0,511},{1,2},{2,1},{3,4},{4,3},{5,6},{6,5},{7,8},{8,7},{9,10},{10... | collective-permute-start | bytes 1228808 | tf_op jit(solution)/shard_map/ppermute | solution.py:20
  68.5 11.9 %collective-permute-start.5 = (f32[800,128]{1,0:T(8,128)S(1)}, f32[800,128]{1,0:T(8,128)S(1)}, u32[]{:S(2)}, u32[]{:S(2)}) collective-permute-start(f32[800,128]{1,0:T(8,128)S(1)} %get-tuple-element.50), channel_id=1, source_target_pairs={{0,1},{1,0},{2,3},{3,2},{4,5},{5,4},{6,7},{7,6},{8,9},{9,8},{10,11... | collective-permute-start | bytes 1228808 | tf_op jit(solution)/shard_map/ppermute | solution.py:25

commit v3 on v2

v3 whole, which is shorter than its diff:
```python
import math

import jax
import jax.numpy as jnp
from jax import lax
from jax.experimental import pallas as pl
from jax.experimental.pallas import tpu as pltpu
from jax.sharding import PartitionSpec as P

BS = 64
AXES = ("blk", "rep")
F32 = jnp.float32
BF16 = jnp.bfloat16
VMEM = pl.BlockSpec(memory_space=pltpu.VMEM)
HBM = pl.BlockSpec(memory_space=pltpu.HBM)


def across(block):
    n = lax.axis_size(AXES)
    return lax.ppermute(block, AXES, [(i, (i + 1 if i % 2 else i - 1) % n) for i in range(n)])


def inside(block):
    n = lax.axis_size(AXES)
    return lax.ppermute(block, AXES, [(i, i ^ 1) for i in range(n)])


def odd():
    return lax.rem(lax.axis_index("rep"), 2) == 1


def zeros(rows, blocks):
    return jnp.zeros((rows, blocks * BS), F32)


def lanes(*parts):
    return jnp.concatenate([p for p in parts if p.shape[1]], axis=1)


def stack(*parts):
    return jnp.concatenate(parts, axis=0)


def split(x):
    high = x.astype(BF16)
    return high, (x - high.astype(F32)).astype(BF16)


def dot(a, b):
    return lax.dot_general(a, b, (((1,), (0,)), ((), ())), preferred_element_type=F32)


def dot3(a_high, a_low, b_high, b_low):
    return dot(a_high, b_high) + (dot(a_high, b_low) + dot(a_low, b_high))


def store(pair, start, value):
    for ref, part in zip(pair, split(value)):
        ref[start : start + value.shape[0], :] = part


def masked_rows(x, mask):
    return stack(*[x[BS * i : BS * (i + 1)] * mask[i : i + 1] for i in range(x.shape[0] // BS)])


def widen(x):
    return stack(*[lanes(zeros(128, 2 * p), x[128 * p : 128 * p + 128], zeros(128, 4 - 2 * p)) for p in range(3)])


def narrow(x):
    return stack(*[x[128 * p : 128 * p + 128, 128 * p : 128 * p + 768] for p in range(3)])


def own_product(left, right):
    out = []
    for p in range(3):
        rows, reach = slice(128 * p, 128 * p + 128), slice(128 * p, 128 * p + 768)
        out.append(dot3(left[0][rows, reach], left[1][rows, reach], right[0][reach, reach], right[1][reach, reach]))
    return widen(stack(*out))


def own_window(x):
    n = x.shape[0] // 6 if x.shape[0] > 8 else 1
    out = [lanes(x[0:n, BS:], zeros(n, 5))]
    for i in range(1, 6):
        out.append(lanes(zeros(n, i - 1), x[n * i : n * (i + 1)], zeros(n, 5 - i)))
    return stack(*out)


def mirror(a, lower):
    br = lax.broadcasted_iota(jnp.int32, a.shape, 0) // BS
    bc = lax.broadcasted_iota(jnp.int32, a.shape, 1) // BS
    keep = br >= bc if lower else br <= bc
    return jnp.where(keep, a, a.T)


def prepare_kernel(h_hbm, pat_hbm, m_ref, mask_ref, b_ref, a_ref, ssq_ref, h_ref, pat_ref, sem):
    fetch_pat = pltpu.make_async_copy(pat_hbm, pat_ref, sem.at[0])
    fetch_h = [
        pltpu.make_async_copy(h_hbm.at[BS * i : BS * (i + 1), :], h_ref.at[BS * i : BS * (i + 1), :], sem.at[1 + i])
        for i in range(6)
    ]
    fetch_pat.start()
    for copy in fetch_h:
        copy.start()
    fetch_pat.wait()
    pat = pat_ref[...].astype(F32)
    owner = lax.broadcasted_iota(jnp.int32, (12, 12 * BS), 1) // BS
    spread = (owner == lax.broadcasted_iota(jnp.int32, (12, 12 * BS), 0)).astype(F32)
    mask = stack(dot(pat, spread), jnp.zeros((2, 12 * BS), F32))
    mask_ref[...] = mask
    side = odd()
    for start, part in ((320, mask[:, 64:448]), (328, lanes(mask[:, 448:768], zeros(8, 1)))):
        b_ref[start : start + 8, :] = part
        a_ref[start : start + 8, :] = part
    total = jnp.zeros((8, 128), F32)
    rows = []
    for i in range(6):
        at = slice(BS * i, BS * (i + 1))
        fetch_h[i].wait()
        row = h_ref[at, :] * mask[i : i + 1, :]
        m_ref[at, :] = row
        square = row * row
        for a in range(8):
            for b in range(6):
                total = total + square[8 * a : 8 * a + 8, 128 * b : 128 * b + 128]
        rows.append(row)
    ssq_ref[...] = jnp.zeros(ssq_ref.shape, F32) + jnp.sum(total)
    for i in range(5):
        at = slice(BS * i, BS * (i + 1))
        to_right, to_left = rows[i + 1][:, 64:448], rows[i][:, 384:768]
        b_ref[at, :] = jnp.where(side, to_right, to_left)
        a_ref[at, :] = jnp.where(side, to_left, to_right)


def copy_all(sem, *pairs):
    copies = [pltpu.make_async_copy(source, target, sem.at[i]) for i, (source, target) in enumerate(pairs)]
    for copy in copies:
        copy.start()
    return copies


def halos(across_ref, inside_ref):
    side = odd()
    fb, fa = across_ref[...], inside_ref[...]
    return jnp.where(side, fa, fb), jnp.where(side, fb, fa)


def surroundings(own, fl, fr, g):
    fl, fr = fl[0:320] * g, fr[0:320] * g
    low = stack(*[lanes(zeros(BS, i), fl[BS * i : BS * (i + 1)], zeros(BS, 4 - i)) for i in range(5)])
    high = stack(*[lanes(zeros(BS, i), fr[BS * i : BS * (i + 1)], zeros(BS, 4 - i)) for i in range(5)])
    cross_l = own[:, 0:384].T[0:320]
    cross_r = own[:, 640:1024].T[64:384]
    hl = lanes(zeros(320, 1), low[:, 0:320], mirror(low[:, 320:640], True), cross_l[:, 0:320])
    hr = lanes(cross_r[:, 64:384], mirror(high[:, 0:320], False), high[:, 320:640], zeros(320, 1))
    return hl, hr


def masks(mask_own, fl, fr):
    mask_l, mask_r = [], []
    for i in range(5):
        band = lanes(fl[321 + i : 322 + i], fl[329 + i : 330 + i, 0:320])
        mask_l.append(lanes(zeros(1, 1 + i), band, zeros(1, 4 - i))[:, 384:1024])
        band = lanes(fr[320 + i : 321 + i], fr[328 + i : 329 + i, 0:320])
        mask_r.append(lanes(zeros(1, i), band, zeros(1, 5 - i))[:, 0:640])
    return own_window(mask_own), stack(*mask_l), stack(*mask_r)


def square_kernel(
    m_ref, mask_ref, b_ref, a_ref, ssq_ref,
    hl_hbm, hr_hbm, s_ref, ko_ref, kl_ref, kr_ref, top_ref, sb_ref, sa_ref, sum_ref,
    oh, ol, wh, wl, hl_ref, hr_ref, sem,
):
    sum_ref[...] = jnp.zeros(sum_ref.shape, F32) + jnp.sum(ssq_ref[...]) / 128.0
    fl, fr = halos(b_ref, a_ref)
    m = m_ref[...]
    top = jnp.maximum(jnp.max(jnp.abs(fl[0:320])), jnp.max(jnp.abs(fr[0:320])))
    top = jnp.maximum(jnp.maximum(top, jnp.max(jnp.abs(m))), 1e-11)
    top_ref[...] = jnp.zeros(top_ref.shape, F32) + top
    mask_o, mask_l, mask_r = masks(mask_ref[...], fl, fr)
    ko_ref[...] = stack(mask_o, jnp.zeros((2, 1024), F32))
    kl_ref[...] = stack(mask_l, jnp.zeros((3, 640), F32))
    kr_ref[...] = stack(mask_r, jnp.zeros((3, 640), F32))
    own = own_window(m) * (1.0 / top)
    hl, hr = surroundings(own, fl, fr, 1.0 / top)
    hl_ref[...] = hl
    hr_ref[...] = hr
    copies = copy_all(sem, (hl_ref, hl_hbm), (hr_ref, hr_hbm))
    store((oh, ol), 0, own)
    store((wh, wl), 0, lanes(hl[:, 384:1024], zeros(320, 6)))
    wh[320:704, :], wl[320:704, :] = oh[...], ol[...]
    store((wh, wl), 704, lanes(zeros(320, 6), hr[:, 0:640]))
    s = masked_rows(own_product((oh, ol), (wh, wl)), mask_o)
    s_ref[...] = narrow(s)
    side = odd()
    scale = zeros(BS, 3) + top
    row = [s[BS * i : BS * (i + 1)] for i in range(6)]
    to_right = stack(
        lanes(row[1][:, 64:384], row[5][:, 320:384]),
        lanes(row[2][:, 128:384], row[4][:, 256:384]),
        lanes(row[3][:, 192:384], scale),
    )
    to_left = stack(
        lanes(row[4][:, 640:960], row[0][:, 640:704]),
        lanes(row[3][:, 640:896], row[1][:, 640:768]),
        lanes(row[2][:, 640:832], scale),
    )
    sb_ref[...] = jnp.where(side, to_right, to_left)
    sa_ref[...] = jnp.where(side, to_left, to_right)
    for copy in copies:
        copy.wait()


def second_kernel(
    norms_ref, top_ref, s_ref, ko_ref, kl_ref, kr_ref, h_hbm, hl_hbm, hr_hbm,
    hl_ref, hr_ref, x_ref, xh, xl, s2_ref, sl_ref, sr_ref, b_ref, a_ref, scal_ref,
    oh, ol, wh, wl, h_ref, sem, *, size
):
    copies = copy_all(sem, (h_hbm, h_ref), (hl_hbm, hl_ref), (hr_hbm, hr_ref))
    s = widen(s_ref[...])
    store((wh, wl), 320, s)
    copies[0].wait()
    own = masked_rows(own_window(h_ref[...]), ko_ref[0:6, :] * (1.0 / top_ref[0:1, 0:1]))
    store((oh, ol), 0, own)
    copies[1].wait()
    hl = hl_ref[...]
    hl_h, hl_l = split(hl)
    far_h, far_l = split(lanes(hl[:, 0:384].T[64:384], zeros(320, 1)))
    none = jnp.zeros((64, 384), BF16)
    right_h = stack(none, far_h, hl_h[:, 384:768], oh[0:320, 0:384])
    right_l = stack(none, far_l, hl_l[:, 384:768], ol[0:320, 0:384])
    s_l = masked_rows(dot3(hl_h, hl_l, right_h, right_l)[:, 0:320], kl_ref[0:5, 0:320])
    sl_ref[...] = s_l
    copies[2].wait()
    hr = hr_ref[...]
    hr_h, hr_l = split(hr)
    far_h, far_l = split(lanes(zeros(320, 1), hr[:, 640:1024].T[0:320]))
    right_h = stack(oh[64:384, 640:1024], hr_h[:, 256:640], far_h, none)
    right_l = stack(ol[64:384, 640:1024], hr_l[:, 256:640], far_l, none)
    s_r = masked_rows(dot3(hr_h, hr_l, right_h, right_l)[:, 64:384], kr_ref[0:5, 320:640])
    sr_ref[...] = s_r

    store((wh, wl), 0, lanes(s_l, s[:, 0:384].T[0:320, 0:320], zeros(320, 6)))
    store((wh, wl), 704, lanes(zeros(320, 6), s[:, 640:1024].T[64:384, 64:384], s_r))
    t_o = masked_rows(own_product((oh, ol), (wh, wl)), ko_ref[0:6, :])
    t_l = dot3(hl_h[:, 384:1024], hl_l[:, 384:1024], wh[0:640, 256:640], wl[0:640, 256:640])
    t_l = masked_rows(t_l[:, 64:384], kl_ref[0:5, 320:640])
    t_r = dot3(hr_h[:, 0:640], hr_l[:, 0:640], wh[384:1024, 384:768], wl[384:1024, 384:768])
    t_r = masked_rows(t_r[:, 0:320], kr_ref[0:5, 0:320])

    frob = jnp.sqrt(jnp.sum(norms_ref[...], keepdims=True)[0] / 128.0)
    inverse = 3.0 * frob / size
    r = top_ref[0:1, 0:1] / inverse
    c1 = 1.5 * r
    c3 = 0.5 * r * r * r
    for i, value in enumerate((inverse, c1, c3)):
        scal_ref[8 * i : 8 * i + 8, :] = jnp.zeros((8, 128), F32) + value
    x = c1 * own - c3 * t_o
    x_ref[...] = x
    store((xh, xl), 0, lanes(zeros(320, 5), c1 * hl[:, 704:1024] - c3 * t_l, zeros(320, 6)))
    store((xh, xl), 320, x)
    store((xh, xl), 704, lanes(zeros(320, 6), c1 * hr[:, 0:320] - c3 * t_r, zeros(320, 5)))
    s2 = []
    for p in range(3):
        rows, reach = slice(320 + 128 * p, 448 + 128 * p), slice(128 * p, 128 * p + 768)
        s2.append(dot3(xh[rows, reach], xl[rows, reach], xh[reach, 256:768], xl[reach, 256:768]))
    s2 = masked_rows(stack(*s2), ko_ref[0:6, 256:768])[:, 64:448]
    s2_ref[...] = s2

    def pack(block):
        tail = lanes(block[0:160, 256:320], block[160:320, 256:320])
        return stack(block[:, 0:128], block[:, 128:256], tail)

    side = odd()
    to_right, to_left = pack(s2[64:384, 64:384]), pack(s2[0:320, 0:320])
    b_ref[...] = jnp.where(side, to_right, to_left)
    a_ref[...] = jnp.where(side, to_left, to_right)


def third_kernel(
    x_ref, xh, xl, s2_ref, hl_ref, hr_ref, s_ref, sl_ref, sr_ref, fb_ref, fa_ref, top_ref, scal_ref, ko_ref, kl_ref, kr_ref,
    out_ref, wh, wl
):
    top = top_ref[0:1, 0:1]
    inverse, c1, c3 = scal_ref[0:1, 0:1], scal_ref[8:9, 0:1], scal_ref[16:17, 0:1]
    fl, fr = halos(fb_ref, fa_ref)
    far_l = stack(
        fl[0:64, 0:320],
        lanes(zeros(BS, 1), fl[64:128, 0:256]),
        lanes(zeros(BS, 2), fl[128:192, 0:192]),
        lanes(zeros(BS, 3), fl[64:128, 256:384]),
        lanes(zeros(BS, 4), fl[0:64, 320:384]),
    )
    far_r = stack(
        lanes(fr[0:64, 320:384], zeros(BS, 4)),
        lanes(fr[64:128, 256:384], zeros(BS, 3)),
        lanes(fr[128:192, 0:192], zeros(BS, 2)),
        lanes(fr[64:128, 0:256], zeros(BS, 1)),
        fr[0:64, 0:320],
    )
    ratio_l, ratio_r = fl[128:129, 192:193] / top, fr[128:129, 192:193] / top
    hl, hr = hl_ref[...], hr_ref[...]
    s = widen(s_ref[...])
    right = stack(zeros(64, 5), (far_l * ratio_l * ratio_l).T, sl_ref[...], s[0:320, 0:320])
    t_l = masked_rows(dot3(*split(hl), *split(right)), kl_ref[0:5, 0:320])
    right = stack(s[64:384, 704:1024], sr_ref[...], (far_r * ratio_r * ratio_r).T, zeros(64, 5))
    t_r = masked_rows(dot3(*split(hr), *split(right)), kr_ref[0:5, 320:640])
    xl_h, xl_l = split(c1 * hl[:, 384:704] - c3 * t_l)
    xr_h, xr_l = split(c1 * hr[:, 320:640] - c3 * t_r)

    ah, al = xh[320:704, :], xl[320:704, :]
    right_h = stack(lanes(xl_h, xh[0:320, 320:384]), xh[320:704, 0:384])
    right_l = stack(lanes(xl_l, xl[0:320, 320:384]), xl[320:704, 0:384])
    s2_a = []
    for p in range(3):
        rows = slice(128 * p, 128 * p + 128)
        part = dot3(ah[rows, 0:704], al[rows, 0:704], right_h[:, 128 * p :], right_l[:, 128 * p :])
        s2_a.append(lanes(zeros(128, 2 * p), part))
    s2_a = masked_rows(stack(*s2_a), ko_ref[0:6, 0:384])
    right_h = stack(xh[320:704, 640:1024], lanes(xh[704:1024, 640:704], xr_h))
    right_l = stack(xl[320:704, 640:1024], lanes(xl[704:1024, 640:704], xr_l))
    s2_b = []
    for p in range(3):
        rows, end = slice(128 * p, 128 * p + 128), 128 * (p + 1)
        part = dot3(ah[rows, 320:1024], al[rows, 320:1024], right_h[:, 0:end], right_l[:, 0:end])
        s2_b.append(lanes(part, zeros(128, 4 - 2 * p)))
    s2_b = masked_rows(stack(*s2_b), ko_ref[0:6, 640:1024])
    left_h, left_l = lanes(xl_h, xh[0:320, 320:640]), lanes(xl_l, xl[0:320, 320:640])
    s2_l = dot3(left_h, left_l, xh[0:640, 256:640], xl[0:640, 256:640])
    s2_l = masked_rows(s2_l[:, 64:384], kl_ref[0:5, 320:640])
    left_h, left_l = lanes(xh[704:1024, 384:704], xr_h), lanes(xl[704:1024, 384:704], xr_l)
    s2_r = dot3(left_h, left_l, xh[384:1024, 384:768], xl[384:1024, 384:768])
    s2_r = masked_rows(s2_r[:, 0:320], kr_ref[0:5, 0:320])
    store((wh, wl), 0, lanes(zeros(320, 5), s2_l, zeros(320, 6)))
    store((wh, wl), 320, lanes(s2_a[:, 0:320], s2_ref[...], s2_b[:, 64:384]))
    store((wh, wl), 704, lanes(zeros(320, 6), s2_r, zeros(320, 5)))
    cubic = own_product((xh.at[320:704, :], xl.at[320:704, :]), (wh, wl))
    for i in range(6):
        at = slice(BS * i, BS * (i + 1))
        row = (1.5 * x_ref[at, :] - 0.5 * (cubic[at] * ko_ref[i : i + 1, :])) * inverse
        if i == 0:
            out_ref[at, :] = lanes(zeros(BS, 1), row[:, 0:704])
        else:
            out_ref[at, :] = row[:, 64 * (i - 1) : 64 * (i - 1) + 768]


def last_kernel(part_ref, xh, xl, ko_ref, scal_ref, fb_ref, fa_ref, out_hbm, out_ref, sem):
    corner_l, corner_r = [
        lanes(f[0:320], f[320:640], stack(f[640:800, 0:64], f[640:800, 64:128]))
        for f in halos(fb_ref, fa_ref)
    ]
    half = 0.5 * scal_ref[0:1, 0:1]
    corner_l = stack(lanes(corner_l, zeros(320, 1)), zeros(64, 6))
    corner_r = stack(zeros(64, 6), lanes(zeros(320, 1), corner_r))
    add_l = dot3(xh[320:640, 0:384], xl[320:640, 0:384], *split(corner_l))
    add_r = dot3(xh[384:704, 640:1024], xl[384:704, 640:1024], *split(corner_r))
    copies = []
    for i in range(6):
        at = slice(BS * i, BS * (i + 1))
        parts = []
        if i < 5:
            part = add_l[at, 64 * i : 320] * (half * ko_ref[i : i + 1, 64 * i : 320])
            parts.append(lanes(zeros(BS, 1), part))
        parts.append(zeros(BS, 12 - (6 - i if i < 5 else 0) - i))
        if i > 0:
            part = add_r[BS * (i - 1) : BS * i, 64 : 64 + 64 * i]
            parts.append(part * (half * ko_ref[i : i + 1, 704 : 704 + 64 * i]))
        out_ref[at, :] = part_ref[at, :] - lanes(*parts)
        copies.append(pltpu.make_async_copy(out_ref.at[at, :], out_hbm.at[at, :], sem.at[i]))
        copies[-1].start()
    for copy in copies:
        copy.wait()


def call(kernel, outs, args, flops, name, mib, scratch=(), in_hbm=(), out_hbm=()):
    args = [pltpu.with_memory_space_constraint(a, pltpu.HBM) if i in in_hbm else a for i, a in enumerate(args)]
    return pl.pallas_call(
        kernel,
        out_shape=[(pltpu.HBM if i in out_hbm else pltpu.VMEM)(s, t) for i, (s, t) in enumerate(outs)],
        in_specs=[HBM if i in in_hbm else VMEM for i in range(len(args))],
        out_specs=[HBM if i in out_hbm else VMEM for i in range(len(outs))],
        scratch_shapes=list(scratch),
        compiler_params=pltpu.CompilerParams(vmem_limit_bytes=mib << 20),
        cost_estimate=pl.CostEstimate(flops=flops, bytes_accessed=1 << 20, transcendentals=0),
        name=name,
    )(*args)


def local(hamiltonian, pattern):
    n_blk, n_rep = lax.axis_size("blk"), lax.axis_size("rep")
    size = math.sqrt(n_blk * n_rep * 6 * BS)
    band = hamiltonian.reshape(6 * BS, 12 * BS)
    own, halo, corner, full = ((384, 1024), F32), ((320, 1024), F32), ((320, 320), F32), ((1024, 1024), BF16)
    mask_o, mask_h, scalar = ((8, 1024), F32), ((8, 640), F32), ((8, 128), F32)
    rows, far = ((384, 1024), BF16), ((192, 384), F32)
    dma = pltpu.SemaphoreType.DMA((2,))

    m, mask, to_b, to_a, ssq = call(
        prepare_kernel,
        [((384, 768), F32), ((8, 768), F32), ((336, 384), F32), ((336, 384), F32), ((n_rep, 1, 128), F32)],
        (band, pattern), 10**7, "prepare", 16,
        scratch=[pltpu.VMEM((384, 768), F32), pltpu.VMEM((6, 12), jnp.int32), pltpu.SemaphoreType.DMA((7,))],
        in_hbm=(0, 1),
    )
    first_b, first_a = across(to_b), inside(to_a)
    ssq = lax.all_to_all(ssq, "rep", 0, 0)
    wide = pltpu.VMEM((1024, 1024), BF16)
    scratch = [pltpu.VMEM(*rows)] * 2 + [wide] * 2
    hl, hr, s, ko, kl, kr, top, to_b, to_a, ssq = call(
        square_kernel,
        [halo, halo, ((384, 768), F32), mask_o, mask_h, mask_h, scalar, far, far, ((n_blk, 1, 128), F32)],
        (m, mask, first_b, first_a, ssq), 10**9, "first_square", 20,
        scratch=scratch + [pltpu.VMEM(*halo), pltpu.VMEM(*halo), dma], out_hbm=(0, 1),
    )
    far_b, far_a = across(to_b), inside(to_a)
    ssq = lax.all_to_all(ssq, "blk", 0, 0)
    hl, hr, x, xh, xl, s2, s_l, s_r, to_b, to_a, scalars = call(
        lambda *refs: second_kernel(*refs, size=size),
        [halo, halo, own, full, full, ((384, 384), F32), corner, corner, ((800, 128), F32), ((800, 128), F32),
         ((24, 128), F32)],
        (ssq, top, s, ko, kl, kr, band, hl, hr), 10**10, "second_square", 24,
        scratch=scratch + [pltpu.VMEM((384, 768), F32), pltpu.SemaphoreType.DMA((3,))], in_hbm=(6, 7, 8),
    )
    from_b, from_a = across(to_b), inside(to_a)
    (part,) = call(
        third_kernel, [((384, 768), F32)],
        (x, xh, xl, s2, hl, hr, s, s_l, s_r, far_b, far_a, top, scalars, ko, kl, kr),
        5 * 10**9, "second_cubic", 24, scratch=[wide, wide],
    )
    (out,) = call(
        last_kernel, [((384, 768), F32)], (part, xh, xl, ko, scalars, from_b, from_a), 10**9, "result", 16,
        scratch=[pltpu.VMEM((384, 768), F32), pltpu.SemaphoreType.DMA((6,))], out_hbm=(0,),
    )
    return out.reshape(6, BS, 12 * BS)


def solution(mesh):
    placed = (P(AXES, None, None), P(AXES, None))
    return jax.shard_map(
        local, mesh=mesh, in_specs=placed, out_specs=P(AXES, None, None), check_vma=False
    )
```

time: 83.1 us -> 78.8 us (0.948)
  the two profiles are of different devices: /device:TPU:2 before, /device:TPU:1 now
where the time goes in v3:
time: 78.8 us; the launch traced here: 78.5 us
  starting transfers between devices  40.8 us (52%)
  Pallas kernels  25.2 us (32%)
  blocking collectives  12.1 us (15%)
    pallas_call x5, Pallas kernels, call(): pl.pallas_call(kernel, out_shape=[(pltpu.HBM if i in out_hbm else pltpu.V...  25.2 us
    ppermute x3, starting transfers between devices, inside(): return lax.ppermute(block, AXES, [(i, i ^ 1) for i in range(n)])  20.7 us
    ppermute x3, starting transfers between devices, across(): lax.ppermute(block, AXES, [(i, (i + 1 if i % 2 else i - 1) % n) for i in...  14.3 us
    all_to_all x1, blocking collectives, local(): ssq = lax.all_to_all(ssq, 'rep', 0, 0)  12.1 us
    all_to_all x1, starting transfers between devices, local(): ssq = lax.all_to_all(ssq, 'blk', 0, 0)  5.76 us
  transfers between devices with their start and end apart: 7, of which 0 were waited for; matrix products, arithmetic and copies ran while one was open for 0% of the time, Pallas kernels for 21%

profile of v3, /device:TPU:1, one launch (start us, length us, event | category | flops | bytes accessed | tf_op | source)
XLA Modules:
  0.0 78.5 jit_solution(6860201972570418727)
XLA Ops:
  0.0 2.2 %prepare.1 = (f32[384,768]{1,0:T(8,128)S(1)}, f32[8,768]{1,0:T(8,128)S(1)}, f32[336,384]{1,0:T(8,128)S(1)}, f32[336,384]{1,0:T(8,128)S(1)}, f32[32,1,128]{2,1,0:T(1,128)S(1)}) custom-call(f32[384,768]{1,0:T(8,128)} %bitcast.2, s32[6,12]{1,0:T(8,128)} %pat_hbm.1), custom_call_target="tpu_custom_call" | custom-call | flops 10000000 | bytes 1048576 | tf_op jit(solution)/shard_map/prepare/pallas_call | solution.py:378
  2.2 6.0 %collective-permute-start = (f32[336,384]{1,0:T(8,128)S(1)}, f32[336,384]{1,0:T(8,128)S(1)}, u32[]{:S(2)}, u32[]{:S(2)}) collective-permute-start(f32[336,384]{1,0:T(8,128)S(1)} %get-tuple-element.33), channel_id=1, source_target_pairs={{0,511},{1,2},{2,1},{3,4},{4,3},{5,6},{6,5},{7,8},{8,7},{9,10},{10... | collective-permute-start | bytes 1548296 | tf_op jit(solution)/shard_map/ppermute | solution.py:20
  8.2 12.9 %collective-permute-start.1 = (f32[336,384]{1,0:T(8,128)S(1)}, f32[336,384]{1,0:T(8,128)S(1)}, u32[]{:S(2)}, u32[]{:S(2)}) collective-permute-start(f32[336,384]{1,0:T(8,128)S(1)} %get-tuple-element.34), channel_id=1, source_target_pairs={{0,1},{1,0},{2,3},{3,2},{4,5},{5,4},{6,7},{7,6},{8,9},{9,8},{10,11... | collective-permute-start | bytes 1548296 | tf_op jit(solution)/shard_map/ppermute | solution.py:25
  21.1 12.1 %all_to_all.10.ssq_ref = f32[32,1,128]{2,1,0:T(1,128)S(1)} all-to-all(f32[32,1,128]{2,1,0:T(1,128)S(1)} %get-tuple-element.35), channel_id=1, replica_groups=mesh['blk'=16,'rep'=32] {'rep'}, dimensions={0} | all-to-all | bytes 32768 | tf_op jit(solution)/shard_map/all_to_all | solution.py:407
  33.2 0.0 collective-permute-done.b_ref
  33.2 0.0 collective-permute-done.1.a_ref
  33.2 4.8 %first_square.1 = (f32[320,1024]{1,0:T(8,128)}, f32[320,1024]{1,0:T(8,128)}, f32[384,768]{1,0:T(8,128)S(1)}, f32[8,1024]{1,0:T(8,128)S(1)}, f32[8,640]{1,0:T(8,1...) custom-call(f32[384,768]{1,0:T(8,128)S(1)} %get-tuple-element.31.m_r, ...), custom_call_target="tpu_custom_call" | custom-call | flops 1000000000 | bytes 1048576 | tf_op jit(solution)/shard_map/first_square/pallas_call | solution.py:378
  38.0 5.8 %all-to-all-start.1 = ((f32[16,1,128]{2,1,0:T(1,128)}), f32[16,1,128]{2,1,0:T(1,128)S(1)}, u32[]{:S(2)}, u32[]{:S(2)}) async-start(f32[16,1,128]{2,1,0:T(1,128)} %get-tuple-element.36), calls=%async_computation.1 | async-start | bytes 16384 | tf_op jit(solution)/shard_map/all_to_all | solution.py:417
  43.8 3.7 %collective-permute-start.2 = (f32[192,384]{1,0:T(8,128)S(1)}, f32[192,384]{1,0:T(8,128)S(1)}, u32[]{:S(2)}, u32[]{:S(2)}) collective-permute-start(f32[192,384]{1,0:T(8,128)S(1)} %get-tuple-element.52), channel_id=1, source_target_pairs={{0,511},{1,2},{2,1},{3,4},{4,3},{5,6},{6,5},{7,8},{8,7},{9,10},{10... | collective-permute-start | bytes 884744 | tf_op jit(solution)/shard_map/ppermute | solution.py:20
  47.5 3.9 %collective-permute-start.3 = (f32[192,384]{1,0:T(8,128)S(1)}, f32[192,384]{1,0:T(8,128)S(1)}, u32[]{:S(2)}, u32[]{:S(2)}) collective-permute-start(f32[192,384]{1,0:T(8,128)S(1)} %get-tuple-element.53), channel_id=1, source_target_pairs={{0,1},{1,0},{2,3},{3,2},{4,5},{5,4},{6,7},{7,6},{8,9},{9,8},{10,11... | collective-permute-start | bytes 884744 | tf_op jit(solution)/shard_map/ppermute | solution.py:25
  51.4 0.0 all-to-all-done.1.refs_0_
  51.4 8.8 %second_square.1 = (f32[320,1024]{1,0:T(8,128)S(1)}, f32[320,1024]{1,0:T(8,128)S(1)}, f32[384,1024]{1,0:T(8,128)S(1)}, bf16[1024,1024]{1,0:T(8,128)(2,1)S(1)}, b...) custom-call(f32[16,1,128]{2,1,0:T(1,128)S(1)} %all-to-all-done.1.ref, ...), custom_call_target="tpu_custom_call" | custom-call | flops 10000000000 | bytes 1048576 | tf_op jit(solution)/shard_map/second_square/pallas_call | solution.py:378
  60.3 4.5 %collective-permute-start.4 = (f32[800,128]{1,0:T(8,128)S(1)}, f32[800,128]{1,0:T(8,128)S(1)}, u32[]{:S(2)}, u32[]{:S(2)}) collective-permute-start(f32[800,128]{1,0:T(8,128)S(1)} %get-tuple-element.55), channel_id=1, source_target_pairs={{0,511},{1,2},{2,1},{3,4},{4,3},{5,6},{6,5},{7,8},{8,7},{9,10},{10... | collective-permute-start | bytes 1228808 | tf_op jit(solution)/shard_map/ppermute | solution.py:20
  64.8 4.0 %collective-permute-start.5 = (f32[800,128]{1,0:T(8,128)S(1)}, f32[800,128]{1,0:T(8,128)S(1)}, u32[]{:S(2)}, u32[]{:S(2)}) collective-permute-start(f32[800,128]{1,0:T(8,128)S(1)} %get-tuple-element.56), channel_id=1, source_target_pairs={{0,1},{1,0},{2,3},{3,2},{4,5},{5,4},{6,7},{7,6},{8,9},{9,8},{10,11... | collective-permute-start | bytes 1228808 | tf_op jit(solution)/shard_map/ppermute | solution.py:25
  68.8 0.0 collective-permute-done.2.fb_ref
  68.8 0.0 collective-permute-done.3.fa_ref
  68.8 7.3 %second_cubic.1.part_ref = f32[384,768]{1,0:T(8,128)S(1)} custom-call(f32[384,1024]{1,0:T(8,128)S(1)} %get-tuple-element.44.x_ref, bf16[1024,1024]{1,0:T(8,128)(2,1)S(1)} %get-tuple-element.45.xh, bf16[1024,1024]{1,0:T(8,128)(2,1)S(1)} %get-tuple-element.46.xl, f32[384,384]{1,0:T(8,128)S(1)} %get-tuple-element.47.s2_ref, ...), custom_call_target="tpu_custom_call" | custom-call | flops 5000000000 | bytes 1048576 | tf_op jit(solution)/shard_map/second_cubic/pallas_call | solution.py:378
  76.1 0.0 collective-permute-done.4.fb_ref
  76.2 0.0 collective-permute-done.5.fa_ref
  76.2 2.1 %result.1 = f32[384,768]{1,0:T(8,128)} custom-call(f32[384,768]{1,0:T(8,128)S(1)} %second_cubic.1.part_ref, bf16[1024,1024]{1,0:T(8,128)(2,1)S(1)} %get-tuple-element.45.xh, bf16[1024,1024]{1,0:T(8,128)(2,1)S(1)} %get-tuple-element.46.xl, f32[8,1024]{1,0:T(8,128)S(1)} %get-tuple-element.39.refs_3_.ko_ref, f32[24,128]{1,0:T(8,128)S(1)} %get-tuple-element.54.scal_ref, ...), custom_call_target="tpu_custom_call" | custom-call | flops 1000000000 | bytes 1048576 | tf_op jit(solution)/shard_map/result/pallas_call | solution.py:378
Async XLA Ops:
  2.2 31.0 %collective-permute-start = (f32[336,384]{1,0:T(8,128)S(1)}, f32[336,384]{1,0:T(8,128)S(1)}, u32[]{:S(2)}, u32[]{:S(2)}) collective-permute-start(f32[336,384]{1,0:T(8,128)S(1)} %get-tuple-element.33), channel_id=1, source_target_pairs={{0,511},{1,2},{2,1},{3,4},{4,3},{5,6},{6,5},{7,8},{8,7},{9,10},{10... | collective-permute-start | bytes 1548296 | tf_op jit(solution)/shard_map/ppermute | solution.py:20
  8.2 25.0 %collective-permute-start.1 = (f32[336,384]{1,0:T(8,128)S(1)}, f32[336,384]{1,0:T(8,128)S(1)}, u32[]{:S(2)}, u32[]{:S(2)}) collective-permute-start(f32[336,384]{1,0:T(8,128)S(1)} %get-tuple-element.34), channel_id=1, source_target_pairs={{0,1},{1,0},{2,3},{3,2},{4,5},{5,4},{6,7},{7,6},{8,9},{9,8},{10,11... | collective-permute-start | bytes 1548296 | tf_op jit(solution)/shard_map/ppermute | solution.py:25
  38.0 13.4 %all-to-all-start.1 = ((f32[16,1,128]{2,1,0:T(1,128)}), f32[16,1,128]{2,1,0:T(1,128)S(1)}, u32[]{:S(2)}, u32[]{:S(2)}) async-start(f32[16,1,128]{2,1,0:T(1,128)} %get-tuple-element.36), calls=%async_computation.1 | async-start | bytes 16384 | tf_op jit(solution)/shard_map/all_to_all | solution.py:417
  43.8 25.0 %collective-permute-start.2 = (f32[192,384]{1,0:T(8,128)S(1)}, f32[192,384]{1,0:T(8,128)S(1)}, u32[]{:S(2)}, u32[]{:S(2)}) collective-permute-start(f32[192,384]{1,0:T(8,128)S(1)} %get-tuple-element.52), channel_id=1, source_target_pairs={{0,511},{1,2},{2,1},{3,4},{4,3},{5,6},{6,5},{7,8},{8,7},{9,10},{10... | collective-permute-start | bytes 884744 | tf_op jit(solution)/shard_map/ppermute | solution.py:20
  47.5 21.3 %collective-permute-start.3 = (f32[192,384]{1,0:T(8,128)S(1)}, f32[192,384]{1,0:T(8,128)S(1)}, u32[]{:S(2)}, u32[]{:S(2)}) collective-permute-start(f32[192,384]{1,0:T(8,128)S(1)} %get-tuple-element.53), channel_id=1, source_target_pairs={{0,1},{1,0},{2,3},{3,2},{4,5},{5,4},{6,7},{7,6},{8,9},{9,8},{10,11... | collective-permute-start | bytes 884744 | tf_op jit(solution)/shard_map/ppermute | solution.py:25
  60.3 15.9 %collective-permute-start.4 = (f32[800,128]{1,0:T(8,128)S(1)}, f32[800,128]{1,0:T(8,128)S(1)}, u32[]{:S(2)}, u32[]{:S(2)}) collective-permute-start(f32[800,128]{1,0:T(8,128)S(1)} %get-tuple-element.55), channel_id=1, source_target_pairs={{0,511},{1,2},{2,1},{3,4},{4,3},{5,6},{6,5},{7,8},{8,7},{9,10},{10... | collective-permute-start | bytes 1228808 | tf_op jit(solution)/shard_map/ppermute | solution.py:20
  64.8 11.3 %collective-permute-start.5 = (f32[800,128]{1,0:T(8,128)S(1)}, f32[800,128]{1,0:T(8,128)S(1)}, u32[]{:S(2)}, u32[]{:S(2)}) collective-permute-start(f32[800,128]{1,0:T(8,128)S(1)} %get-tuple-element.56), channel_id=1, source_target_pairs={{0,1},{1,0},{2,3},{3,2},{4,5},{5,4},{6,7},{7,6},{8,9},{9,8},{10,11... | collective-permute-start | bytes 1228808 | tf_op jit(solution)/shard_map/ppermute | solution.py:25

commit v4 on v3

--- a/solution.py
+++ b/solution.py
@@ -52,6 +52,28 @@
 
 def dot3(a_high, a_low, b_high, b_low):
     return dot(a_high, b_high) + (dot(a_high, b_low) + dot(a_low, b_high))
+
+
+def cross_left(left, right):
+    (lh, ll), (rh, rl) = left, right
+    upper = dot3(lh[0:192, 0:512], ll[0:192, 0:512], rh[0:512, 256:512], rl[0:512, 256:512])
+    lower = dot3(lh[192:320, :], ll[192:320, :], rh[0:640, 256:640], rl[0:640, 256:640])
+    return stack(lanes(upper[:, 64:256], zeros(192, 2)), lower[:, 64:384])
+
+
+def cross_right(left, right):
+    (lh, ll), (rh, rl) = left, right
+    upper = dot3(lh[0:128, :], ll[0:128, :], rh[384:1024, 384:768], rl[384:1024, 384:768])
+    lower = dot3(lh[128:320, 128:640], ll[128:320, 128:640], rh[512:1024, 512:768], rl[512:1024, 512:768])
+    return stack(upper[:, 0:320], lanes(zeros(192, 2), lower[:, 0:192]))
+
+
+def gram(high, low):
+    def times(a, b):
+        return lax.dot_general(a, b, (((1,), (1,)), ((), ())), preferred_element_type=F32)
+
+    mixed = times(high, low)
+    return times(high, high) + (mixed + mixed.T)
 
 
 def store(pair, start, value):
@@ -214,8 +236,8 @@
 
 def second_kernel(
     norms_ref, top_ref, s_ref, ko_ref, kl_ref, kr_ref, h_hbm, hl_hbm, hr_hbm,
-    hl_ref, hr_ref, x_ref, xh, xl, s2_ref, sl_ref, sr_ref, b_ref, a_ref, scal_ref,
-    oh, ol, wh, wl, h_ref, sem, *, size
+    hl_h, hl_l, hr_h, hr_l, wh, wl, near_l, near_r, x_ref, xh, xl, s2_ref, b_ref, a_ref, scal_ref,
+    oh, ol, hl_ref, hr_ref, h_ref, sem, *, size
 ):
     copies = copy_all(sem, (h_hbm, h_ref), (hl_hbm, hl_ref), (hr_hbm, hr_ref))
     s = widen(s_ref[...])
@@ -225,29 +247,22 @@
     store((oh, ol), 0, own)
     copies[1].wait()
     hl = hl_ref[...]
-    hl_h, hl_l = split(hl)
-    far_h, far_l = split(lanes(hl[:, 0:384].T[64:384], zeros(320, 1)))
-    none = jnp.zeros((64, 384), BF16)
-    right_h = stack(none, far_h, hl_h[:, 384:768], oh[0:320, 0:384])
-    right_l = stack(none, far_l, hl_l[:, 384:768], ol[0:320, 0:384])
-    s_l = masked_rows(dot3(hl_h, hl_l, right_h, right_l)[:, 0:320], kl_ref[0:5, 0:320])
-    sl_ref[...] = s_l
+    store((hl_h, hl_l), 0, hl)
+    s_l = masked_rows(gram(hl_h[...], hl_l[...]), kl_ref[0:5, 0:320])
     copies[2].wait()
     hr = hr_ref[...]
-    hr_h, hr_l = split(hr)
-    far_h, far_l = split(lanes(zeros(320, 1), hr[:, 640:1024].T[0:320]))
-    right_h = stack(oh[64:384, 640:1024], hr_h[:, 256:640], far_h, none)
-    right_l = stack(ol[64:384, 640:1024], hr_l[:, 256:640], far_l, none)
-    s_r = masked_rows(dot3(hr_h, hr_l, right_h, right_l)[:, 64:384], kr_ref[0:5, 320:640])
-    sr_ref[...] = s_r
+    store((hr_h, hr_l), 0, hr)
+    s_r = masked_rows(gram(hr_h[...], hr_l[...]), kr_ref[0:5, 320:640])
 
     store((wh, wl), 0, lanes(s_l, s[:, 0:384].T[0:320, 0:320], zeros(320, 6)))
     store((wh, wl), 704, lanes(zeros(320, 6), s[:, 640:1024].T[64:384, 64:384], s_r))
     t_o = masked_rows(own_product((oh, ol), (wh, wl)), ko_ref[0:6, :])
-    t_l = dot3(hl_h[:, 384:1024], hl_l[:, 384:1024], wh[0:640, 256:640], wl[0:640, 256:640])
-    t_l = masked_rows(t_l[:, 64:384], kl_ref[0:5, 320:640])
-    t_r = dot3(hr_h[:, 0:640], hr_l[:, 0:640], wh[384:1024, 384:768], wl[384:1024, 384:768])
-    t_r = masked_rows(t_r[:, 0:320], kr_ref[0:5, 0:320])
+    near_l[...] = hl[:, 384:704]
+    near_r[...] = hr[:, 320:640]
+    t_l = cross_left((hl_h[:, 384:1024], hl_l[:, 384:1024]), (wh, wl))
+    t_l = masked_rows(t_l, kl_ref[0:5, 320:640])
+    t_r = cross_right((hr_h[:, 0:640], hr_l[:, 0:640]), (wh, wl))
+    t_r = masked_rows(t_r, kr_ref[0:5, 0:320])
 
     frob = jnp.sqrt(jnp.sum(norms_ref[...], keepdims=True)[0] / 128.0)
     inverse = 3.0 * frob / size
@@ -279,8 +294,8 @@
 
 
 def third_kernel(
-    x_ref, xh, xl, s2_ref, hl_ref, hr_ref, s_ref, sl_ref, sr_ref, fb_ref, fa_ref, top_ref, scal_ref, ko_ref, kl_ref, kr_ref,
-    out_ref, wh, wl
+    x_ref, xh, xl, s2_ref, hl_h, hl_l, hr_h, hr_l, sh, sl, near_l, near_r, fb_ref, fa_ref, top_ref, scal_ref,
+    ko_ref, kl_ref, kr_ref, out_ref, wh, wl
 ):
     top = top_ref[0:1, 0:1]
     inverse, c1, c3 = scal_ref[0:1, 0:1], scal_ref[8:9, 0:1], scal_ref[16:17, 0:1]
@@ -300,38 +315,37 @@
         fr[0:64, 0:320],
     )
     ratio_l, ratio_r = fl[128:129, 192:193] / top, fr[128:129, 192:193] / top
-    hl, hr = hl_ref[...], hr_ref[...]
-    s = widen(s_ref[...])
-    right = stack(zeros(64, 5), (far_l * ratio_l * ratio_l).T, sl_ref[...], s[0:320, 0:320])
-    t_l = masked_rows(dot3(*split(hl), *split(right)), kl_ref[0:5, 0:320])
-    right = stack(s[64:384, 704:1024], sr_ref[...], (far_r * ratio_r * ratio_r).T, zeros(64, 5))
-    t_r = masked_rows(dot3(*split(hr), *split(right)), kr_ref[0:5, 320:640])
-    xl_h, xl_l = split(c1 * hl[:, 384:704] - c3 * t_l)
-    xr_h, xr_l = split(c1 * hr[:, 320:640] - c3 * t_r)
+    far_h, far_s = split(stack(zeros(64, 6), lanes((far_l * ratio_l * ratio_l).T, zeros(320, 1))))
+    right_h, right_l = stack(far_h, sh[0:640, 0:384]), stack(far_s, sl[0:640, 0:384])
+    t_l = dot3(hl_h[...], hl_l[...], right_h, right_l)[:, 0:320]
+    far_h, far_s = split(stack(lanes(zeros(320, 1), (far_r * ratio_r * ratio_r).T), zeros(64, 6)))
+    right_h, right_l = stack(sh[384:1024, 640:1024], far_h), stack(sl[384:1024, 640:1024], far_s)
+    t_r = dot3(hr_h[...], hr_l[...], right_h, right_l)[:, 64:384]
+    xl_h, xl_l = split(c1 * near_l[...] - c3 * masked_rows(t_l, kl_ref[0:5, 0:320]))
+    xr_h, xr_l = split(c1 * near_r[...] - c3 * masked_rows(t_r, kr_ref[0:5, 320:640]))
 
     ah, al = xh[320:704, :], xl[320:704, :]
     right_h = stack(lanes(xl_h, xh[0:320, 320:384]), xh[320:704, 0:384])
     right_l = stack(lanes(xl_l, xl[0:320, 320:384]), xl[320:704, 0:384])
     s2_a = []
     for p in range(3):
-        rows = slice(128 * p, 128 * p + 128)
-        part = dot3(ah[rows, 0:704], al[rows, 0:704], right_h[:, 128 * p :], right_l[:, 128 * p :])
+        rows, reach = slice(128 * p, 128 * p + 128), slice(128 * p, 640)
+        part = dot3(ah[rows, reach], al[rows, reach], right_h[reach, 128 * p :], right_l[reach, 128 * p :])
         s2_a.append(lanes(zeros(128, 2 * p), part))
     s2_a = masked_rows(stack(*s2_a), ko_ref[0:6, 0:384])
     right_h = stack(xh[320:704, 640:1024], lanes(xh[704:1024, 640:704], xr_h))
     right_l = stack(xl[320:704, 640:1024], lanes(xl[704:1024, 640:704], xr_l))
     s2_b = []
     for p in range(3):
-        rows, end = slice(128 * p, 128 * p + 128), 128 * (p + 1)
-        part = dot3(ah[rows, 320:1024], al[rows, 320:1024], right_h[:, 0:end], right_l[:, 0:end])
+        rows, reach, end = slice(128 * p, 128 * p + 128), slice(384, 768 + 128 * p), 128 * (p + 1)
+        inner = slice(64, 448 + 128 * p)
+        part = dot3(ah[rows, reach], al[rows, reach], right_h[inner, 0:end], right_l[inner, 0:end])
         s2_b.append(lanes(part, zeros(128, 4 - 2 * p)))
     s2_b = masked_rows(stack(*s2_b), ko_ref[0:6, 640:1024])
     left_h, left_l = lanes(xl_h, xh[0:320, 320:640]), lanes(xl_l, xl[0:320, 320:640])
-    s2_l = dot3(left_h, left_l, xh[0:640, 256:640], xl[0:640, 256:640])
-    s2_l = masked_rows(s2_l[:, 64:384], kl_ref[0:5, 320:640])
+    s2_l = masked_rows(cross_left((left_h, left_l), (xh, xl)), kl_ref[0:5, 320:640])
     left_h, left_l = lanes(xh[704:1024, 384:704], xr_h), lanes(xl[704:1024, 384:704], xr_l)
-    s2_r = dot3(left_h, left_l, xh[384:1024, 384:768], xl[384:1024, 384:768])
-    s2_r = masked_rows(s2_r[:, 0:320], kr_ref[0:5, 0:320])
+    s2_r = masked_rows(cross_right((left_h, left_l), (xh, xl)), kr_ref[0:5, 0:320])
     store((wh, wl), 0, lanes(zeros(320, 5), s2_l, zeros(320, 6)))
     store((wh, wl), 320, lanes(s2_a[:, 0:320], s2_ref[...], s2_b[:, 64:384]))
     store((wh, wl), 704, lanes(zeros(320, 6), s2_r, zeros(320, 5)))
@@ -353,8 +367,12 @@
     half = 0.5 * scal_ref[0:1, 0:1]
     corner_l = stack(lanes(corner_l, zeros(320, 1)), zeros(64, 6))
     corner_r = stack(zeros(64, 6), lanes(zeros(320, 1), corner_r))
-    add_l = dot3(xh[320:640, 0:384], xl[320:640, 0:384], *split(corner_l))
-    add_r = dot3(xh[384:704, 640:1024], xl[384:704, 640:1024], *split(corner_r))
+    ch, cl = split(corner_l)
+    near = dot3(xh[448:640, 128:384], xl[448:640, 128:384], ch[128:384, 128:384], cl[128:384, 128:384])
+    add_l = stack(dot3(xh[320:448, 0:384], xl[320:448, 0:384], ch, cl), lanes(zeros(192, 2), near))
+    ch, cl = split(corner_r)
+    near = dot3(xh[384:576, 640:896], xl[384:576, 640:896], ch[0:256, 0:256], cl[0:256, 0:256])
+    add_r = stack(lanes(near, zeros(192, 2)), dot3(xh[576:704, 640:1024], xl[576:704, 640:1024], ch, cl))
     copies = []
     for i in range(6):
         at = slice(BS * i, BS * (i + 1))
@@ -406,26 +424,28 @@
     first_b, first_a = across(to_b), inside(to_a)
     ssq = lax.all_to_all(ssq, "rep", 0, 0)
     wide = pltpu.VMEM((1024, 1024), BF16)
-    scratch = [pltpu.VMEM(*rows)] * 2 + [wide] * 2
     hl, hr, s, ko, kl, kr, top, to_b, to_a, ssq = call(
         square_kernel,
         [halo, halo, ((384, 768), F32), mask_o, mask_h, mask_h, scalar, far, far, ((n_blk, 1, 128), F32)],
         (m, mask, first_b, first_a, ssq), 10**9, "first_square", 20,
-        scratch=scratch + [pltpu.VMEM(*halo), pltpu.VMEM(*halo), dma], out_hbm=(0, 1),
+        scratch=[pltpu.VMEM(*rows)] * 2 + [wide] * 2 + [pltpu.VMEM(*halo), pltpu.VMEM(*halo), dma], out_hbm=(0, 1),
     )
     far_b, far_a = across(to_b), inside(to_a)
     ssq = lax.all_to_all(ssq, "blk", 0, 0)
-    hl, hr, x, xh, xl, s2, s_l, s_r, to_b, to_a, scalars = call(
+    pair = ((320, 1024), BF16)
+    *operands, x, xh, xl, s2, to_b, to_a, scalars = call(
         lambda *refs: second_kernel(*refs, size=size),
-        [halo, halo, own, full, full, ((384, 384), F32), corner, corner, ((800, 128), F32), ((800, 128), F32),
-         ((24, 128), F32)],
+        [pair, pair, pair, pair, full, full, corner, corner, own, full, full, ((384, 384), F32),
+         ((800, 128), F32), ((800, 128), F32), ((24, 128), F32)],
         (ssq, top, s, ko, kl, kr, band, hl, hr), 10**10, "second_square", 24,
-        scratch=scratch + [pltpu.VMEM((384, 768), F32), pltpu.SemaphoreType.DMA((3,))], in_hbm=(6, 7, 8),
+        scratch=[pltpu.VMEM(*rows)] * 2 + [pltpu.VMEM(*halo)] * 2
+        + [pltpu.VMEM((384, 768), F32), pltpu.SemaphoreType.DMA((3,))],
+        in_hbm=(6, 7, 8),
     )
     from_b, from_a = across(to_b), inside(to_a)
     (part,) = call(
         third_kernel, [((384, 768), F32)],
-        (x, xh, xl, s2, hl, hr, s, s_l, s_r, far_b, far_a, top, scalars, ko, kl, kr),
+        (x, xh, xl, s2, *operands, far_b, far_a, top, scalars, ko, kl, kr),
         5 * 10**9, "second_cubic", 24, scratch=[wide, wide],
     )
     (out,) = call(

time: 78.8 us -> 76.8 us (0.975)
  Pallas kernels: 25.2 us -> 23.4 us
    pallas_call x5, Pallas kernels: 25.2 us -> 23.4 us  [call(): pl.pallas_call(kernel, out_shape=[(pltpu.HBM if i in out_hbm else pltpu.V...]
  transfers between devices with their start and end apart: 7 -> 7, of which waited for: 0 -> 0; matrix products, arithmetic and copies ran while one was open for 0% -> 0% of each run, Pallas kernels for 21% -> 19%
where the time goes in v4:
time: 76.8 us; the launch traced here: 76.4 us
  starting transfers between devices  40.6 us (53%)
  Pallas kernels  23.4 us (30%)
  blocking collectives  12.1 us (16%)
    pallas_call x5, Pallas kernels, call(): pl.pallas_call(kernel, out_shape=[(pltpu.HBM if i in out_hbm else pltpu.V...  23.4 us
    ppermute x3, starting transfers between devices, inside(): return lax.ppermute(block, AXES, [(i, i ^ 1) for i in range(n)])  20.3 us
    ppermute x3, starting transfers between devices, across(): lax.ppermute(block, AXES, [(i, (i + 1 if i % 2 else i - 1) % n) for i in...  14.5 us
    all_to_all x1, blocking collectives, local(): ssq = lax.all_to_all(ssq, 'rep', 0, 0)  12.1 us
    all_to_all x1, starting transfers between devices, local(): ssq = lax.all_to_all(ssq, 'blk', 0, 0)  5.76 us
  transfers between devices with their start and end apart: 7, of which 0 were waited for; matrix products, arithmetic and copies ran while one was open for 0% of the time, Pallas kernels for 19%

profile of v4, /device:TPU:1, one launch (start us, length us, event | category | flops | bytes accessed | tf_op | source)
XLA Modules:
  0.0 76.4 jit_solution(15843847946061534328)
XLA Ops:
  0.0 2.2 %prepare.1 = (f32[384,768]{1,0:T(8,128)S(1)}, f32[8,768]{1,0:T(8,128)S(1)}, f32[336,384]{1,0:T(8,128)S(1)}, f32[336,384]{1,0:T(8,128)S(1)}, f32[32,1,128]{2,1,0:T(1,128)S(1)}) custom-call(f32[384,768]{1,0:T(8,128)} %bitcast.2, s32[6,12]{1,0:T(8,128)} %pat_hbm.1), custom_call_target="tpu_custom_call" | custom-call | flops 10000000 | bytes 1048576 | tf_op jit(solution)/shard_map/prepare/pallas_call | solution.py:396
  2.2 6.0 %collective-permute-start = (f32[336,384]{1,0:T(8,128)S(1)}, f32[336,384]{1,0:T(8,128)S(1)}, u32[]{:S(2)}, u32[]{:S(2)}) collective-permute-start(f32[336,384]{1,0:T(8,128)S(1)} %get-tuple-element.37), channel_id=1, source_target_pairs={{0,511},{1,2},{2,1},{3,4},{4,3},{5,6},{6,5},{7,8},{8,7},{9,10},{10... | collective-permute-start | bytes 1548296 | tf_op jit(solution)/shard_map/ppermute | solution.py:20
  8.2 12.9 %collective-permute-start.1 = (f32[336,384]{1,0:T(8,128)S(1)}, f32[336,384]{1,0:T(8,128)S(1)}, u32[]{:S(2)}, u32[]{:S(2)}) collective-permute-start(f32[336,384]{1,0:T(8,128)S(1)} %get-tuple-element.38), channel_id=1, source_target_pairs={{0,1},{1,0},{2,3},{3,2},{4,5},{5,4},{6,7},{7,6},{8,9},{9,8},{10,11... | collective-permute-start | bytes 1548296 | tf_op jit(solution)/shard_map/ppermute | solution.py:25
  21.1 12.1 %all_to_all.10.ssq_ref = f32[32,1,128]{2,1,0:T(1,128)S(1)} all-to-all(f32[32,1,128]{2,1,0:T(1,128)S(1)} %get-tuple-element.39), channel_id=1, replica_groups=mesh['blk'=16,'rep'=32] {'rep'}, dimensions={0} | all-to-all | bytes 32768 | tf_op jit(solution)/shard_map/all_to_all | solution.py:425
  33.2 0.0 collective-permute-done.b_ref
  33.2 0.0 collective-permute-done.1.a_ref
  33.2 4.8 %first_square.1 = (f32[320,1024]{1,0:T(8,128)}, f32[320,1024]{1,0:T(8,128)}, f32[384,768]{1,0:T(8,128)S(1)}, f32[8,1024]{1,0:T(8,128)S(1)}, f32[8,640]{1,0:T(8,1...) custom-call(f32[384,768]{1,0:T(8,128)S(1)} %get-tuple-element.35.m_r, ...), custom_call_target="tpu_custom_call" | custom-call | flops 1000000000 | bytes 1048576 | tf_op jit(solution)/shard_map/first_square/pallas_call | solution.py:396
  38.0 5.8 %all-to-all-start.1 = ((f32[16,1,128]{2,1,0:T(1,128)}), f32[16,1,128]{2,1,0:T(1,128)S(1)}, u32[]{:S(2)}, u32[]{:S(2)}) async-start(f32[16,1,128]{2,1,0:T(1,128)} %get-tuple-element.40), calls=%async_computation.1 | async-start | bytes 16384 | tf_op jit(solution)/shard_map/all_to_all | solution.py:434
  43.8 3.7 %collective-permute-start.2 = (f32[192,384]{1,0:T(8,128)S(1)}, f32[192,384]{1,0:T(8,128)S(1)}, u32[]{:S(2)}, u32[]{:S(2)}) collective-permute-start(f32[192,384]{1,0:T(8,128)S(1)} %get-tuple-element.60), channel_id=1, source_target_pairs={{0,511},{1,2},{2,1},{3,4},{4,3},{5,6},{6,5},{7,8},{8,7},{9,10},{10... | collective-permute-start | bytes 884744 | tf_op jit(solution)/shard_map/ppermute | solution.py:20
  47.5 3.7 %collective-permute-start.3 = (f32[192,384]{1,0:T(8,128)S(1)}, f32[192,384]{1,0:T(8,128)S(1)}, u32[]{:S(2)}, u32[]{:S(2)}) collective-permute-start(f32[192,384]{1,0:T(8,128)S(1)} %get-tuple-element.61), channel_id=1, source_target_pairs={{0,1},{1,0},{2,3},{3,2},{4,5},{5,4},{6,7},{7,6},{8,9},{9,8},{10,11... | collective-permute-start | bytes 884744 | tf_op jit(solution)/shard_map/ppermute | solution.py:25
  51.2 0.0 all-to-all-done.1.refs_0_
  51.2 8.4 %second_square.1 = (bf16[320,1024]{1,0:T(8,128)(2,1)S(1)}, bf16[320,1024]{1,0:T(8,128)(2,1)S(1)}, bf16[320,1024]{1,0:T(8,128)(2,1)S(1)}, bf16[320,1024]{1,0:T(8,...) custom-call(f32[16,1,128]{2,1,0:T(1,128)S(1)} %all-to-all-done.1.ref, ...), custom_call_target="tpu_custom_call" | custom-call | flops 10000000000 | bytes 1048576 | tf_op jit(solution)/shard_map/second_square/pallas_call | solution.py:396
  59.6 4.7 %collective-permute-start.4 = (f32[800,128]{1,0:T(8,128)S(1)}, f32[800,128]{1,0:T(8,128)S(1)}, u32[]{:S(2)}, u32[]{:S(2)}) collective-permute-start(f32[800,128]{1,0:T(8,128)S(1)} %get-tuple-element.63), channel_id=1, source_target_pairs={{0,511},{1,2},{2,1},{3,4},{4,3},{5,6},{6,5},{7,8},{8,7},{9,10},{10... | collective-permute-start | bytes 1228808 | tf_op jit(solution)/shard_map/ppermute | solution.py:20
  64.3 3.8 %collective-permute-start.5 = (f32[800,128]{1,0:T(8,128)S(1)}, f32[800,128]{1,0:T(8,128)S(1)}, u32[]{:S(2)}, u32[]{:S(2)}) collective-permute-start(f32[800,128]{1,0:T(8,128)S(1)} %get-tuple-element.64), channel_id=1, source_target_pairs={{0,1},{1,0},{2,3},{3,2},{4,5},{5,4},{6,7},{7,6},{8,9},{9,8},{10,11... | collective-permute-start | bytes 1228808 | tf_op jit(solution)/shard_map/ppermute | solution.py:25
  68.1 0.0 collective-permute-done.2.fb_ref
  68.1 0.0 collective-permute-done.3.fa_ref
  68.1 6.4 %second_cubic.1.part_ref = f32[384,768]{1,0:T(8,128)S(1)} custom-call(f32[384,1024]{1,0:T(8,128)S(1)} %get-tuple-element.48.x_ref, bf16[1024,1024]{1,0:T(8,128)(2,1)S(1)} %get-tuple-element.49.xh, bf16[1024,1024]{1,0:T(8,128)(2,1)S(1)} %get-tuple-element.50.xl, f32[384,384]{1,0:T(8,128)S(1)} %get-tuple-element.51.s2_ref, ...), custom_call_target="tpu_custom_call" | custom-call | flops 5000000000 | bytes 1048576 | tf_op jit(solution)/shard_map/second_cubic/pallas_call | solution.py:396
  74.5 0.0 collective-permute-done.4.fb_ref
  74.5 0.0 collective-permute-done.5.fa_ref
  74.5 1.7 %result.1 = f32[384,768]{1,0:T(8,128)} custom-call(f32[384,768]{1,0:T(8,128)S(1)} %second_cubic.1.part_ref, bf16[1024,1024]{1,0:T(8,128)(2,1)S(1)} %get-tuple-element.49.xh, bf16[1024,1024]{1,0:T(8,128)(2,1)S(1)} %get-tuple-element.50.xl, f32[8,1024]{1,0:T(8,128)S(1)} %get-tuple-element.43.refs_3_.ko_ref, f32[24,128]{1,0:T(8,128)S(1)} %get-tuple-element.62.scal_ref, ...), custom_call_target="tpu_custom_call" | custom-call | flops 1000000000 | bytes 1048576 | tf_op jit(solution)/shard_map/result/pallas_call | solution.py:396
Async XLA Ops:
  2.2 31.0 %collective-permute-start = (f32[336,384]{1,0:T(8,128)S(1)}, f32[336,384]{1,0:T(8,128)S(1)}, u32[]{:S(2)}, u32[]{:S(2)}) collective-permute-start(f32[336,384]{1,0:T(8,128)S(1)} %get-tuple-element.37), channel_id=1, source_target_pairs={{0,511},{1,2},{2,1},{3,4},{4,3},{5,6},{6,5},{7,8},{8,7},{9,10},{10... | collective-permute-start | bytes 1548296 | tf_op jit(solution)/shard_map/ppermute | solution.py:20
  8.2 25.0 %collective-permute-start.1 = (f32[336,384]{1,0:T(8,128)S(1)}, f32[336,384]{1,0:T(8,128)S(1)}, u32[]{:S(2)}, u32[]{:S(2)}) collective-permute-start(f32[336,384]{1,0:T(8,128)S(1)} %get-tuple-element.38), channel_id=1, source_target_pairs={{0,1},{1,0},{2,3},{3,2},{4,5},{5,4},{6,7},{7,6},{8,9},{9,8},{10,11... | collective-permute-start | bytes 1548296 | tf_op jit(solution)/shard_map/ppermute | solution.py:25
  38.0 13.2 %all-to-all-start.1 = ((f32[16,1,128]{2,1,0:T(1,128)}), f32[16,1,128]{2,1,0:T(1,128)S(1)}, u32[]{:S(2)}, u32[]{:S(2)}) async-start(f32[16,1,128]{2,1,0:T(1,128)} %get-tuple-element.40), calls=%async_computation.1 | async-start | bytes 16384 | tf_op jit(solution)/shard_map/all_to_all | solution.py:434
  43.8 24.3 %collective-permute-start.2 = (f32[192,384]{1,0:T(8,128)S(1)}, f32[192,384]{1,0:T(8,128)S(1)}, u32[]{:S(2)}, u32[]{:S(2)}) collective-permute-start(f32[192,384]{1,0:T(8,128)S(1)} %get-tuple-element.60), channel_id=1, source_target_pairs={{0,511},{1,2},{2,1},{3,4},{4,3},{5,6},{6,5},{7,8},{8,7},{9,10},{10... | collective-permute-start | bytes 884744 | tf_op jit(solution)/shard_map/ppermute | solution.py:20
  47.5 20.6 %collective-permute-start.3 = (f32[192,384]{1,0:T(8,128)S(1)}, f32[192,384]{1,0:T(8,128)S(1)}, u32[]{:S(2)}, u32[]{:S(2)}) collective-permute-start(f32[192,384]{1,0:T(8,128)S(1)} %get-tuple-element.61), channel_id=1, source_target_pairs={{0,1},{1,0},{2,3},{3,2},{4,5},{5,4},{6,7},{7,6},{8,9},{9,8},{10,11... | collective-permute-start | bytes 884744 | tf_op jit(solution)/shard_map/ppermute | solution.py:25
  59.6 14.9 %collective-permute-start.4 = (f32[800,128]{1,0:T(8,128)S(1)}, f32[800,128]{1,0:T(8,128)S(1)}, u32[]{:S(2)}, u32[]{:S(2)}) collective-permute-start(f32[800,128]{1,0:T(8,128)S(1)} %get-tuple-element.63), channel_id=1, source_target_pairs={{0,511},{1,2},{2,1},{3,4},{4,3},{5,6},{6,5},{7,8},{8,7},{9,10},{10... | collective-permute-start | bytes 1228808 | tf_op jit(solution)/shard_map/ppermute | solution.py:20
  64.3 10.2 %collective-permute-start.5 = (f32[800,128]{1,0:T(8,128)S(1)}, f32[800,128]{1,0:T(8,128)S(1)}, u32[]{:S(2)}, u32[]{:S(2)}) collective-permute-start(f32[800,128]{1,0:T(8,128)S(1)} %get-tuple-element.64), channel_id=1, source_target_pairs={{0,1},{1,0},{2,3},{3,2},{4,5},{5,4},{6,7},{7,6},{8,9},{9,8},{10,11... | collective-permute-start | bytes 1228808 | tf_op jit(solution)/shard_map/ppermute | solution.py:25

commit v5 on v4

--- a/solution.py
+++ b/solution.py
@@ -77,8 +77,9 @@
 
 
 def store(pair, start, value):
-    for ref, part in zip(pair, split(value)):
-        ref[start : start + value.shape[0], :] = part
+    for at in range(0, value.shape[0], 32):
+        for ref, part in zip(pair, split(value[at : at + 32])):
+            ref[start + at : start + at + 32, :] = part
 
 
 def masked_rows(x, mask):

time: 76.8 us -> 76.7 us (level)
  no operation moved by 1% of the time
where the time goes in v5:
time: 76.7 us; the launch traced here: 76.3 us
  starting transfers between devices  40.6 us (53%)
  Pallas kernels  23.4 us (31%)
  blocking collectives  12.1 us (16%)
    pallas_call x5, Pallas kernels, call(): pl.pallas_call(kernel, out_shape=[(pltpu.HBM if i in out_hbm else pltpu.V...  23.4 us
    ppermute x3, starting transfers between devices, inside(): return lax.ppermute(block, AXES, [(i, i ^ 1) for i in range(n)])  20.3 us
    ppermute x3, starting transfers between devices, across(): lax.ppermute(block, AXES, [(i, (i + 1 if i % 2 else i - 1) % n) for i in...  14.5 us
    all_to_all x1, blocking collectives, local(): ssq = lax.all_to_all(ssq, 'rep', 0, 0)  12.1 us
    all_to_all x1, starting transfers between devices, local(): ssq = lax.all_to_all(ssq, 'blk', 0, 0)  5.77 us
  transfers between devices with their start and end apart: 7, of which 0 were waited for; matrix products, arithmetic and copies ran while one was open for 0% of the time, Pallas kernels for 19%

profile of v5, /device:TPU:1, one launch (start us, length us, event | category | flops | bytes accessed | tf_op | source)
XLA Modules:
  0.0 76.3 jit_solution(3384275241797340830)
XLA Ops:
  0.0 2.2 %prepare.1 = (f32[384,768]{1,0:T(8,128)S(1)}, f32[8,768]{1,0:T(8,128)S(1)}, f32[336,384]{1,0:T(8,128)S(1)}, f32[336,384]{1,0:T(8,128)S(1)}, f32[32,1,128]{2,1,0:T(1,128)S(1)}) custom-call(f32[384,768]{1,0:T(8,128)} %bitcast.2, s32[6,12]{1,0:T(8,128)} %pat_hbm.1), custom_call_target="tpu_custom_call" | custom-call | flops 10000000 | bytes 1048576 | tf_op jit(solution)/shard_map/prepare/pallas_call | solution.py:397
  2.2 6.0 %collective-permute-start = (f32[336,384]{1,0:T(8,128)S(1)}, f32[336,384]{1,0:T(8,128)S(1)}, u32[]{:S(2)}, u32[]{:S(2)}) collective-permute-start(f32[336,384]{1,0:T(8,128)S(1)} %get-tuple-element.37), channel_id=1, source_target_pairs={{0,511},{1,2},{2,1},{3,4},{4,3},{5,6},{6,5},{7,8},{8,7},{9,10},{10... | collective-permute-start | bytes 1548296 | tf_op jit(solution)/shard_map/ppermute | solution.py:20
  8.2 12.9 %collective-permute-start.1 = (f32[336,384]{1,0:T(8,128)S(1)}, f32[336,384]{1,0:T(8,128)S(1)}, u32[]{:S(2)}, u32[]{:S(2)}) collective-permute-start(f32[336,384]{1,0:T(8,128)S(1)} %get-tuple-element.38), channel_id=1, source_target_pairs={{0,1},{1,0},{2,3},{3,2},{4,5},{5,4},{6,7},{7,6},{8,9},{9,8},{10,11... | collective-permute-start | bytes 1548296 | tf_op jit(solution)/shard_map/ppermute | solution.py:25
  21.1 12.1 %all_to_all.10.ssq_ref = f32[32,1,128]{2,1,0:T(1,128)S(1)} all-to-all(f32[32,1,128]{2,1,0:T(1,128)S(1)} %get-tuple-element.39), channel_id=1, replica_groups=mesh['blk'=16,'rep'=32] {'rep'}, dimensions={0} | all-to-all | bytes 32768 | tf_op jit(solution)/shard_map/all_to_all | solution.py:426
  33.2 0.0 collective-permute-done.b_ref
  33.2 0.0 collective-permute-done.1.a_ref
  33.2 4.8 %first_square.1 = (f32[320,1024]{1,0:T(8,128)}, f32[320,1024]{1,0:T(8,128)}, f32[384,768]{1,0:T(8,128)S(1)}, f32[8,1024]{1,0:T(8,128)S(1)}, f32[8,640]{1,0:T(8,1...) custom-call(f32[384,768]{1,0:T(8,128)S(1)} %get-tuple-element.35.m_r, ...), custom_call_target="tpu_custom_call" | custom-call | flops 1000000000 | bytes 1048576 | tf_op jit(solution)/shard_map/first_square/pallas_call | solution.py:397
  38.0 5.8 %all-to-all-start.1 = ((f32[16,1,128]{2,1,0:T(1,128)}), f32[16,1,128]{2,1,0:T(1,128)S(1)}, u32[]{:S(2)}, u32[]{:S(2)}) async-start(f32[16,1,128]{2,1,0:T(1,128)} %get-tuple-element.40), calls=%async_computation.1 | async-start | bytes 16384 | tf_op jit(solution)/shard_map/all_to_all | solution.py:435
  43.8 3.7 %collective-permute-start.2 = (f32[192,384]{1,0:T(8,128)S(1)}, f32[192,384]{1,0:T(8,128)S(1)}, u32[]{:S(2)}, u32[]{:S(2)}) collective-permute-start(f32[192,384]{1,0:T(8,128)S(1)} %get-tuple-element.60), channel_id=1, source_target_pairs={{0,511},{1,2},{2,1},{3,4},{4,3},{5,6},{6,5},{7,8},{8,7},{9,10},{10... | collective-permute-start | bytes 884744 | tf_op jit(solution)/shard_map/ppermute | solution.py:20
  47.5 3.7 %collective-permute-start.3 = (f32[192,384]{1,0:T(8,128)S(1)}, f32[192,384]{1,0:T(8,128)S(1)}, u32[]{:S(2)}, u32[]{:S(2)}) collective-permute-start(f32[192,384]{1,0:T(8,128)S(1)} %get-tuple-element.61), channel_id=1, source_target_pairs={{0,1},{1,0},{2,3},{3,2},{4,5},{5,4},{6,7},{7,6},{8,9},{9,8},{10,11... | collective-permute-start | bytes 884744 | tf_op jit(solution)/shard_map/ppermute | solution.py:25
  51.2 0.0 all-to-all-done.1.refs_0_
  51.2 8.3 %second_square.1 = (bf16[320,1024]{1,0:T(8,128)(2,1)S(1)}, bf16[320,1024]{1,0:T(8,128)(2,1)S(1)}, bf16[320,1024]{1,0:T(8,128)(2,1)S(1)}, bf16[320,1024]{1,0:T(8,...) custom-call(f32[16,1,128]{2,1,0:T(1,128)S(1)} %all-to-all-done.1.ref, ...), custom_call_target="tpu_custom_call" | custom-call | flops 10000000000 | bytes 1048576 | tf_op jit(solution)/shard_map/second_square/pallas_call | solution.py:397
  59.5 4.7 %collective-permute-start.4 = (f32[800,128]{1,0:T(8,128)S(1)}, f32[800,128]{1,0:T(8,128)S(1)}, u32[]{:S(2)}, u32[]{:S(2)}) collective-permute-start(f32[800,128]{1,0:T(8,128)S(1)} %get-tuple-element.63), channel_id=1, source_target_pairs={{0,511},{1,2},{2,1},{3,4},{4,3},{5,6},{6,5},{7,8},{8,7},{9,10},{10... | collective-permute-start | bytes 1228808 | tf_op jit(solution)/shard_map/ppermute | solution.py:20
  64.3 3.8 %collective-permute-start.5 = (f32[800,128]{1,0:T(8,128)S(1)}, f32[800,128]{1,0:T(8,128)S(1)}, u32[]{:S(2)}, u32[]{:S(2)}) collective-permute-start(f32[800,128]{1,0:T(8,128)S(1)} %get-tuple-element.64), channel_id=1, source_target_pairs={{0,1},{1,0},{2,3},{3,2},{4,5},{5,4},{6,7},{7,6},{8,9},{9,8},{10,11... | collective-permute-start | bytes 1228808 | tf_op jit(solution)/shard_map/ppermute | solution.py:25
  68.0 0.0 collective-permute-done.2.fb_ref
  68.1 0.0 collective-permute-done.3.fa_ref
  68.1 6.4 %second_cubic.1.part_ref = f32[384,768]{1,0:T(8,128)S(1)} custom-call(f32[384,1024]{1,0:T(8,128)S(1)} %get-tuple-element.48.x_ref, bf16[1024,1024]{1,0:T(8,128)(2,1)S(1)} %get-tuple-element.49.xh, bf16[1024,1024]{1,0:T(8,128)(2,1)S(1)} %get-tuple-element.50.xl, f32[384,384]{1,0:T(8,128)S(1)} %get-tuple-element.51.s2_ref, ...), custom_call_target="tpu_custom_call" | custom-call | flops 5000000000 | bytes 1048576 | tf_op jit(solution)/shard_map/second_cubic/pallas_call | solution.py:397
  74.4 0.0 collective-permute-done.4.fb_ref
  74.5 0.0 collective-permute-done.5.fa_ref
  74.5 1.7 %result.1 = f32[384,768]{1,0:T(8,128)} custom-call(f32[384,768]{1,0:T(8,128)S(1)} %second_cubic.1.part_ref, bf16[1024,1024]{1,0:T(8,128)(2,1)S(1)} %get-tuple-element.49.xh, bf16[1024,1024]{1,0:T(8,128)(2,1)S(1)} %get-tuple-element.50.xl, f32[8,1024]{1,0:T(8,128)S(1)} %get-tuple-element.43.refs_3_.ko_ref, f32[24,128]{1,0:T(8,128)S(1)} %get-tuple-element.62.scal_ref, ...), custom_call_target="tpu_custom_call" | custom-call | flops 1000000000 | bytes 1048576 | tf_op jit(solution)/shard_map/result/pallas_call | solution.py:397
Async XLA Ops:
  2.2 31.0 %collective-permute-start = (f32[336,384]{1,0:T(8,128)S(1)}, f32[336,384]{1,0:T(8,128)S(1)}, u32[]{:S(2)}, u32[]{:S(2)}) collective-permute-start(f32[336,384]{1,0:T(8,128)S(1)} %get-tuple-element.37), channel_id=1, source_target_pairs={{0,511},{1,2},{2,1},{3,4},{4,3},{5,6},{6,5},{7,8},{8,7},{9,10},{10... | collective-permute-start | bytes 1548296 | tf_op jit(solution)/shard_map/ppermute | solution.py:20
  8.2 25.0 %collective-permute-start.1 = (f32[336,384]{1,0:T(8,128)S(1)}, f32[336,384]{1,0:T(8,128)S(1)}, u32[]{:S(2)}, u32[]{:S(2)}) collective-permute-start(f32[336,384]{1,0:T(8,128)S(1)} %get-tuple-element.38), channel_id=1, source_target_pairs={{0,1},{1,0},{2,3},{3,2},{4,5},{5,4},{6,7},{7,6},{8,9},{9,8},{10,11... | collective-permute-start | bytes 1548296 | tf_op jit(solution)/shard_map/ppermute | solution.py:25
  38.0 13.2 %all-to-all-start.1 = ((f32[16,1,128]{2,1,0:T(1,128)}), f32[16,1,128]{2,1,0:T(1,128)S(1)}, u32[]{:S(2)}, u32[]{:S(2)}) async-start(f32[16,1,128]{2,1,0:T(1,128)} %get-tuple-element.40), calls=%async_computation.1 | async-start | bytes 16384 | tf_op jit(solution)/shard_map/all_to_all | solution.py:435
  43.8 24.3 %collective-permute-start.2 = (f32[192,384]{1,0:T(8,128)S(1)}, f32[192,384]{1,0:T(8,128)S(1)}, u32[]{:S(2)}, u32[]{:S(2)}) collective-permute-start(f32[192,384]{1,0:T(8,128)S(1)} %get-tuple-element.60), channel_id=1, source_target_pairs={{0,511},{1,2},{2,1},{3,4},{4,3},{5,6},{6,5},{7,8},{8,7},{9,10},{10... | collective-permute-start | bytes 884744 | tf_op jit(solution)/shard_map/ppermute | solution.py:20
  47.5 20.6 %collective-permute-start.3 = (f32[192,384]{1,0:T(8,128)S(1)}, f32[192,384]{1,0:T(8,128)S(1)}, u32[]{:S(2)}, u32[]{:S(2)}) collective-permute-start(f32[192,384]{1,0:T(8,128)S(1)} %get-tuple-element.61), channel_id=1, source_target_pairs={{0,1},{1,0},{2,3},{3,2},{4,5},{5,4},{6,7},{7,6},{8,9},{9,8},{10,11... | collective-permute-start | bytes 884744 | tf_op jit(solution)/shard_map/ppermute | solution.py:25
  59.5 14.9 %collective-permute-start.4 = (f32[800,128]{1,0:T(8,128)S(1)}, f32[800,128]{1,0:T(8,128)S(1)}, u32[]{:S(2)}, u32[]{:S(2)}) collective-permute-start(f32[800,128]{1,0:T(8,128)S(1)} %get-tuple-element.63), channel_id=1, source_target_pairs={{0,511},{1,2},{2,1},{3,4},{4,3},{5,6},{6,5},{7,8},{8,7},{9,10},{10... | collective-permute-start | bytes 1228808 | tf_op jit(solution)/shard_map/ppermute | solution.py:20
  64.3 10.2 %collective-permute-start.5 = (f32[800,128]{1,0:T(8,128)S(1)}, f32[800,128]{1,0:T(8,128)S(1)}, u32[]{:S(2)}, u32[]{:S(2)}) collective-permute-start(f32[800,128]{1,0:T(8,128)S(1)} %get-tuple-element.64), channel_id=1, source_target_pairs={{0,1},{1,0},{2,3},{3,2},{4,5},{5,4},{6,7},{7,6},{8,9},{9,8},{10,11... | collective-permute-start | bytes 1228808 | tf_op jit(solution)/shard_map/ppermute | solution.py:25
